TPU v7x, 32 devices: a whole 2x2x4 slice. The times are simulated.
32 devices in a mesh: ctx: 8 (over y, x, core), fsdp: 4 (over z).
Axes of the slice: x: 2, y: 2, z: 4, core: 2. Of those that a mesh axis runs over, the one named last changes fastest.
Arguments:
- tokens: bfloat16 [16, 1024, 768], P('fsdp', 'ctx'), may hold values from -6 to 6
- cotangent: bfloat16 [16, 1024, 768], P('fsdp', 'ctx'), may hold values from -6 to 6
- lengths: int32 [16], P('fsdp'), may hold values from 256 to 1024, as said below
- bucket_table: int32 [2047], replicated, may hold values from 0 to 31, as said below
- gain_attn: bfloat16 [768], P('fsdp'), may hold values from 0.5 to 1.5
- w_query: bfloat16 [768, 768], P('fsdp'), may hold values from -0.109375 to 0.109375
- w_key: bfloat16 [768, 768], P('fsdp'), may hold values from -0.109375 to 0.109375
- w_value: bfloat16 [768, 768], P('fsdp'), may hold values from -0.21875 to 0.21875
- w_out: bfloat16 [768, 768], P('fsdp'), may hold values from -6 to 6
- bias_table: bfloat16 [32, 12], P('fsdp'), may hold values from -4 to 4
- gain_ffn: bfloat16 [768], P('fsdp'), may hold values from 0.5 to 1.5
- w_gate: bfloat16 [768, 3072], P('fsdp'), may hold values from -0.21875 to 0.21875
- w_up: bfloat16 [768, 3072], P('fsdp'), may hold values from -0.21875 to 0.21875
- w_ffn_out: bfloat16 [3072, 768], P('fsdp'), may hold values from -0.109375 to 0.109375
Outputs:
- out: bfloat16 [16, 1024, 768], P('fsdp', 'ctx')
- grad_tokens: float32 [16, 1024, 768], P('fsdp', 'ctx')
- grad_gain_attn: float32 [768], P('fsdp')
- grad_w_query: float32 [768, 768], P('fsdp')
- grad_w_key: float32 [768, 768], P('fsdp')
- grad_w_value: float32 [768, 768], P('fsdp')
- grad_w_out: float32 [768, 768], P('fsdp')
- grad_bias_table: float32 [32, 12], P('fsdp')
- grad_gain_ffn: float32 [768], P('fsdp')
- grad_w_gate: float32 [768, 3072], P('fsdp')
- grad_w_up: float32 [768, 3072], P('fsdp')
- grad_w_ffn_out: float32 [3072, 768], P('fsdp')
Inputs may be any that keep to these rules, and one draw needn't show every extreme that they name: `lengths`: of the 4 sequences of each index of fsdp (consecutive sequences), one has 1024 used slots and one a quarter of 1024. `bucket_table`: entry r + 1023 is the bucket of a key r slots after its query; it depends on |r| and the sign of r only, equals |r| for |r| < 32 // 4 (plus 32 // 2 where r > 0) and never falls as |r| grows.
All inputs are finite; a program needn't handle non-finite values.
Results may differ from a plain program's by a relative error of at most 0.02.
Values may be sent and summed in bfloat16 or wider, within the bound.
No kernel may reach another device: no remote copies, remote signals or barrier semaphores. Data moves between devices by JAX's collectives and lax.ppermute only.
A program may use at most 256 MiB of HBM per device.

v0:
```python
import math

import jax
import jax.numpy as jnp
from jax import lax
from jax.sharding import PartitionSpec as P

HEADS = 12
HEAD_DIM = 64
BUCKETS = 32


norm_eps = 1e-06


def gelu_tanh(values):
    return (
        0.5
        * values
        * (1.0 + jnp.tanh(0.7978845608028654 * (values + 0.044715 * values * values * values)))
    )


def normalize(values, gain_vec):
    return (
        values * lax.rsqrt(jnp.mean(values * values, axis=-1, keepdims=True) + norm_eps) * gain_vec
    )


def project(values, matrix):
    return jnp.einsum("msd,de->mse", values, matrix, preferred_element_type=jnp.float32)


def back_project(values, matrix):
    return jnp.einsum("mse,de->msd", values, matrix, preferred_element_type=jnp.float32)


def outer_sum(left_rows, right_rows):
    return jnp.einsum("msd,mse->de", left_rows, right_rows, preferred_element_type=jnp.float32)


def split_heads(values):
    return values.reshape(values.shape[0], values.shape[1], HEADS, HEAD_DIM)


def toeplitz_bias(offset_bias, start, query_rows, key_rows):
    span = query_rows + key_rows - 1
    window = lax.dynamic_slice_in_dim(offset_bias, start, span, 1)
    wrapped = jnp.concatenate(
        [
            window[:, query_rows - 1 :],
            jnp.zeros((window.shape[0], 1), jnp.float32),
            window[:, : query_rows - 1],
        ],
        axis=1,
    )
    tiled = jnp.tile(wrapped, (1, query_rows))
    shaped = tiled[:, : query_rows * span].reshape(window.shape[0], query_rows, span)
    return shaped[:, :, :key_rows]


def diagonal_sums(grad_bias, query_rows, key_rows):
    span = query_rows + key_rows - 1
    heads = grad_bias.shape[0]
    padded = jnp.pad(grad_bias, ((0, 0), (0, 0), (0, span - key_rows)))
    flat = jnp.pad(padded.reshape(heads, query_rows * span), ((0, 0), (0, query_rows)))
    slots = jnp.sum(flat.reshape(heads, query_rows, span + 1), axis=1)
    return jnp.concatenate([slots[:, key_rows + 1 :], slots[:, :key_rows]], axis=1)


def block_scores(query_heads, key_heads, pair_bias, key_ok):
    scores = jnp.einsum(
        "mihe,mjhe->mhij", query_heads, key_heads, preferred_element_type=jnp.float32
    )
    scores = scores + pair_bias[None]
    return jnp.where(key_ok[:, None, None, :], scores, -1e30)


def over_blocks(update, make_bias, carried, pieces):
    piece_rows = pieces[0].shape[1]
    block_rows = math.gcd(piece_rows, 256)
    block_count = piece_rows // block_rows

    def advance(block_index, running):
        block_start = block_index * block_rows
        sub_pieces = tuple(
            (
                lax.dynamic_slice_in_dim(member, block_index * block_rows, block_rows, 1)
                for member in pieces
            )
        )
        bias_info = make_bias(block_start, block_rows)
        return update(running, sub_pieces, block_start, slice(None), bias_info)

    return lax.fori_loop(0, block_count, advance, carried)


def per_device(
    tokens,
    cotangent,
    lengths,
    bucket_table,
    gain_attn,
    w_query,
    w_key,
    w_value,
    w_out,
    bias_table,
    gain_ffn,
    w_gate,
    w_up,
    w_ffn_out,
):
    shards = (
        gain_attn,
        w_query,
        w_key,
        w_value,
        w_out,
        bias_table,
        gain_ffn,
        w_gate,
        w_up,
        w_ffn_out,
    )
    gathered = (
        lax.all_gather(shards[0], "fsdp", axis=0, tiled=True),
        lax.all_gather(shards[1], "fsdp", axis=0, tiled=True),
        lax.all_gather(shards[2], "fsdp", axis=0, tiled=True),
        lax.all_gather(shards[3], "fsdp", axis=0, tiled=True),
        lax.all_gather(shards[4], "fsdp", axis=0, tiled=True),
        lax.all_gather(shards[5], "fsdp", axis=0, tiled=True),
        lax.all_gather(shards[6], "fsdp", axis=0, tiled=True),
        lax.all_gather(shards[7], "fsdp", axis=0, tiled=True),
        lax.all_gather(shards[8], "fsdp", axis=0, tiled=True),
        lax.all_gather(shards[9], "fsdp", axis=0, tiled=True),
    )
    (
        full_gain_attn,
        full_query,
        full_key,
        full_value,
        full_out,
        full_bias,
        full_gain_ffn,
        full_gate,
        full_up,
        full_ffn_out,
    ) = gathered
    batch_rows, local_rows, model_width = tokens.shape
    seq_len = local_rows * lax.axis_size("ctx")
    table_len = bucket_table.shape[0]
    first_pos = lax.axis_index("ctx") * local_rows
    positions = first_pos + jnp.arange(local_rows, dtype=jnp.int32)
    valid_mask = positions[None, :] < lengths[:, None]
    valid_rows = valid_mask.astype(jnp.float32)
    bucket_hot = bucket_table[:, None] == jnp.arange(BUCKETS, dtype=jnp.int32)[None, :]

    def offset_bias_of(bias_weights):
        return jnp.einsum(
            "tb,bh->ht",
            bucket_hot.astype(jnp.bfloat16),
            bias_weights,
            preferred_element_type=jnp.float32,
        )

    forward_offsets = offset_bias_of(full_bias)

    def keys_bias(offset_bias):

        def keys_make(block_start, block_rows):
            start = block_start - first_pos - (local_rows - 1) + (seq_len - 1)
            return (toeplitz_bias(offset_bias, start, local_rows, block_rows), start)

        return keys_make

    def queries_bias(offset_bias):

        def queries_make(block_start, block_rows):
            start = first_pos - block_start - (block_rows - 1) + (seq_len - 1)
            return (toeplitz_bias(offset_bias, start, block_rows, local_rows), start)

        return queries_make

    tokens_f = tokens.astype(jnp.float32)
    attn_gain = full_gain_attn.astype(jnp.float32)
    normed = normalize(tokens_f, attn_gain).astype(jnp.bfloat16)
    queries = project(normed, full_query).astype(jnp.bfloat16)
    keys_local = project(normed, full_key).astype(jnp.bfloat16)
    values_local = project(normed, full_value).astype(jnp.bfloat16)
    query_heads = split_heads(queries)

    def forward_block(running, sub_pieces, block_start, member_pick, bias_info):
        max_score, row_total, weighted = running
        key_part, value_part = sub_pieces
        key_pos = block_start + jnp.arange(key_part.shape[1], dtype=jnp.int32)
        key_ok = key_pos[None, :] < lengths[:, None]
        scores = block_scores(query_heads, split_heads(key_part), bias_info[0], key_ok)
        new_max = jnp.maximum(max_score, jnp.max(scores, axis=-1))
        shrink = jnp.exp(max_score - new_max)
        weights = jnp.exp(scores - new_max[..., None])
        row_total = row_total * shrink + jnp.sum(weights, axis=-1)
        weighted = weighted * jnp.transpose(shrink, (0, 2, 1))[..., None] + jnp.einsum(
            "mhij,mjhe->mihe",
            weights.astype(jnp.bfloat16),
            split_heads(value_part),
            preferred_element_type=jnp.float32,
        )
        return (new_max, row_total, weighted)

    start_state = (
        jnp.full((batch_rows, HEADS, local_rows), -1e30, jnp.float32),
        jnp.zeros((batch_rows, HEADS, local_rows), jnp.float32),
        jnp.zeros((batch_rows, local_rows, HEADS, HEAD_DIM), jnp.float32),
    )
    max_score, row_total, weighted = over_blocks(
        forward_block,
        keys_bias(forward_offsets),
        start_state,
        (
            lax.all_gather(keys_local, "ctx", axis=1, tiled=True),
            lax.all_gather(values_local, "ctx", axis=1, tiled=True),
        ),
    )
    log_total = max_score + jnp.log(row_total)
    attn_full = weighted / jnp.transpose(row_total, (0, 2, 1))[..., None]
    attn_low = attn_full.reshape(batch_rows, local_rows, model_width).astype(jnp.bfloat16)
    residual = tokens_f + project(attn_low, full_out)
    ffn_gain = full_gain_ffn.astype(jnp.float32)
    normed_ffn = normalize(residual, ffn_gain).astype(jnp.bfloat16)
    gate_proj = project(normed_ffn, full_gate)
    up_proj = project(normed_ffn, full_up)
    hidden = (gelu_tanh(gate_proj) * up_proj).astype(jnp.bfloat16)
    result = valid_rows[..., None] * (residual + project(hidden, full_ffn_out))
    output = result.astype(jnp.bfloat16)
    back_weights = (
        lax.all_gather(shards[0], "fsdp", axis=0, tiled=True),
        lax.all_gather(shards[1], "fsdp", axis=0, tiled=True),
        lax.all_gather(shards[2], "fsdp", axis=0, tiled=True),
        lax.all_gather(shards[3], "fsdp", axis=0, tiled=True),
        lax.all_gather(shards[4], "fsdp", axis=0, tiled=True),
        lax.all_gather(shards[5], "fsdp", axis=0, tiled=True),
        lax.all_gather(shards[6], "fsdp", axis=0, tiled=True),
        lax.all_gather(shards[7], "fsdp", axis=0, tiled=True),
        lax.all_gather(shards[8], "fsdp", axis=0, tiled=True),
        lax.all_gather(shards[9], "fsdp", axis=0, tiled=True),
    )
    (
        back_gain_attn,
        back_query,
        back_key,
        back_value,
        back_out,
        back_bias,
        back_gain_ffn,
        back_gate,
        back_up,
        back_ffn_out,
    ) = back_weights
    back_offsets = offset_bias_of(back_bias)
    grad_out = cotangent.astype(jnp.float32) * valid_rows[..., None]
    grad_low = grad_out.astype(jnp.bfloat16)
    grad_w_ffn_out = outer_sum(hidden, grad_low)
    grad_hidden = back_project(grad_low, back_ffn_out)

    def gated_product(gate_in, up_in):
        return gelu_tanh(gate_in) * up_in

    gated_value, gated_back = jax.vjp(gated_product, gate_proj, up_proj)
    grad_gate, grad_up = gated_back(grad_hidden)
    grad_gate = grad_gate.astype(jnp.bfloat16)
    grad_up = grad_up.astype(jnp.bfloat16)
    grad_w_gate = outer_sum(normed_ffn, grad_gate)
    grad_w_up = outer_sum(normed_ffn, grad_up)
    grad_normed_ffn = back_project(grad_gate, back_gate) + back_project(grad_up, back_up)
    norm_value, norm_back = jax.vjp(normalize, residual, back_gain_ffn.astype(jnp.float32))
    grad_resid_part, grad_gain_ffn = norm_back(grad_normed_ffn)
    grad_resid = grad_out + grad_resid_part
    grad_branch = grad_resid.astype(jnp.bfloat16)
    grad_w_out = outer_sum(attn_low, grad_branch)
    grad_attn = back_project(grad_branch, back_out).astype(jnp.bfloat16)
    grad_heads = split_heads(grad_attn)
    delta_row = jnp.einsum(
        "mihe,mihe->mhi", grad_heads, attn_full, preferred_element_type=jnp.float32
    )

    def query_grad_block(running, sub_pieces, block_start, member_pick, bias_info):
        grad_query, grad_offsets = running
        pair_bias, table_start = bias_info
        key_part, value_part = sub_pieces
        key_heads = split_heads(key_part)
        key_pos = block_start + jnp.arange(key_part.shape[1], dtype=jnp.int32)
        key_ok = key_pos[None, :] < lengths[:, None]
        scores = block_scores(query_heads, key_heads, pair_bias, key_ok)
        probabilities = jnp.exp(scores - log_total[..., None])
        grad_probs = jnp.einsum(
            "mihe,mjhe->mhij",
            grad_heads,
            split_heads(value_part),
            preferred_element_type=jnp.float32,
        )
        grad_scores = (probabilities * (grad_probs - delta_row[..., None])).astype(jnp.bfloat16)
        grad_query = grad_query + jnp.einsum(
            "mhij,mjhe->mihe", grad_scores, key_heads, preferred_element_type=jnp.float32
        )
        pair_grad = jnp.sum(grad_scores.astype(jnp.float32), axis=0)
        diag = diagonal_sums(pair_grad, pair_grad.shape[1], pair_grad.shape[2])
        current = lax.dynamic_slice_in_dim(grad_offsets, table_start, diag.shape[1], 1)
        grad_offsets = lax.dynamic_update_slice_in_dim(grad_offsets, current + diag, table_start, 1)
        return (grad_query, grad_offsets)

    query_state = (
        jnp.zeros((batch_rows, local_rows, HEADS, HEAD_DIM), jnp.float32),
        jnp.zeros((HEADS, table_len), jnp.float32),
    )
    grad_query, grad_offsets = over_blocks(
        query_grad_block,
        keys_bias(back_offsets),
        query_state,
        (
            lax.all_gather(keys_local, "ctx", axis=1, tiled=True),
            lax.all_gather(values_local, "ctx", axis=1, tiled=True),
        ),
    )
    grad_buckets = jnp.einsum(
        "ht,tb->bh", grad_offsets, bucket_hot.astype(jnp.float32), precision=lax.Precision.HIGHEST
    )
    stats_lse, stats_delta = (
        lax.all_gather(log_total, "ctx", axis=2, tiled=True),
        lax.all_gather(delta_row, "ctx", axis=2, tiled=True),
    )
    key_heads_local = split_heads(keys_local)
    value_heads_local = split_heads(values_local)

    def key_grad_block(running, sub_pieces, block_start, member_pick, bias_info):
        grad_key, grad_value = running
        query_part, grad_part = sub_pieces
        rows_here = query_part.shape[1]
        query_part_heads = split_heads(query_part)
        grad_part_heads = split_heads(grad_part)
        scores = block_scores(query_part_heads, key_heads_local, bias_info[0], valid_mask)
        lse_part = lax.dynamic_slice_in_dim(stats_lse, block_start, rows_here, 2)
        delta_part = lax.dynamic_slice_in_dim(stats_delta, block_start, rows_here, 2)
        probabilities = jnp.exp(scores - lse_part[..., None])
        grad_value = grad_value + jnp.einsum(
            "mhij,mihe->mjhe",
            probabilities.astype(jnp.bfloat16),
            grad_part_heads,
            preferred_element_type=jnp.float32,
        )
        grad_probs = jnp.einsum(
            "mihe,mjhe->mhij",
            grad_part_heads,
            value_heads_local,
            preferred_element_type=jnp.float32,
        )
        grad_scores = (probabilities * (grad_probs - delta_part[..., None])).astype(jnp.bfloat16)
        grad_key = grad_key + jnp.einsum(
            "mhij,mihe->mjhe", grad_scores, query_part_heads, preferred_element_type=jnp.float32
        )
        return (grad_key, grad_value)

    key_state = (
        jnp.zeros((batch_rows, local_rows, HEADS, HEAD_DIM), jnp.float32),
        jnp.zeros((batch_rows, local_rows, HEADS, HEAD_DIM), jnp.float32),
    )
    grad_key, grad_value = over_blocks(
        key_grad_block,
        queries_bias(back_offsets),
        key_state,
        (
            lax.all_gather(queries, "ctx", axis=1, tiled=True),
            lax.all_gather(grad_attn, "ctx", axis=1, tiled=True),
        ),
    )
    grad_q = grad_query.reshape(batch_rows, local_rows, model_width).astype(jnp.bfloat16)
    grad_k = grad_key.reshape(batch_rows, local_rows, model_width).astype(jnp.bfloat16)
    grad_v = grad_value.reshape(batch_rows, local_rows, model_width).astype(jnp.bfloat16)
    grad_w_query = outer_sum(normed, grad_q)
    grad_w_key = outer_sum(normed, grad_k)
    grad_w_value = outer_sum(normed, grad_v)
    grad_normed = (
        back_project(grad_q, back_query)
        + back_project(grad_k, back_key)
        + back_project(grad_v, back_value)
    )
    attn_norm_value, attn_norm_back = jax.vjp(
        normalize, tokens_f, back_gain_attn.astype(jnp.float32)
    )
    grad_tokens_part, grad_gain_attn = attn_norm_back(grad_normed)
    grad_tokens = grad_resid + grad_tokens_part
    grads = (
        grad_gain_attn,
        grad_w_query,
        grad_w_key,
        grad_w_value,
        grad_w_out,
        grad_buckets,
        grad_gain_ffn,
        grad_w_gate,
        grad_w_up,
        grad_w_ffn_out,
    )
    shard_sums = (
        lax.psum_scatter(grads[0], "fsdp", scatter_dimension=0, tiled=True),
        lax.psum_scatter(grads[1], "fsdp", scatter_dimension=0, tiled=True),
        lax.psum_scatter(grads[2], "fsdp", scatter_dimension=0, tiled=True),
        lax.psum_scatter(grads[3], "fsdp", scatter_dimension=0, tiled=True),
        lax.psum_scatter(grads[4], "fsdp", scatter_dimension=0, tiled=True),
        lax.psum_scatter(grads[5], "fsdp", scatter_dimension=0, tiled=True),
        lax.psum_scatter(grads[6], "fsdp", scatter_dimension=0, tiled=True),
        lax.psum_scatter(grads[7], "fsdp", scatter_dimension=0, tiled=True),
        lax.psum_scatter(grads[8], "fsdp", scatter_dimension=0, tiled=True),
        lax.psum_scatter(grads[9], "fsdp", scatter_dimension=0, tiled=True),
    )
    totals = lax.psum(
        (
            shard_sums[0],
            shard_sums[1],
            shard_sums[2],
            shard_sums[3],
            shard_sums[4],
            shard_sums[5],
            shard_sums[6],
            shard_sums[7],
            shard_sums[8],
            shard_sums[9],
        ),
        "ctx",
    )
    return (output, grad_tokens) + tuple(totals)


def solution(mesh):
    placed = (
        P("fsdp", "ctx", None),
        P("fsdp", "ctx", None),
        P("fsdp"),
        P(),
        P("fsdp"),
        P("fsdp", None),
        P("fsdp", None),
        P("fsdp", None),
        P("fsdp", None),
        P("fsdp", None),
        P("fsdp"),
        P("fsdp", None),
        P("fsdp", None),
        P("fsdp", None),
    )
    return jax.shard_map(
        per_device,
        mesh=mesh,
        in_specs=placed,
        out_specs=(
            P("fsdp", "ctx", None),
            P("fsdp", "ctx", None),
            P("fsdp"),
            P("fsdp", None),
            P("fsdp", None),
            P("fsdp", None),
            P("fsdp", None),
            P("fsdp", None),
            P("fsdp"),
            P("fsdp", None),
            P("fsdp", None),
            P("fsdp", None),
        ),
        check_vma=False,
    )
```

profile of v0, /device:TPU:9, one launch (start us, length us, event | category | flops | bytes accessed | tf_op | source)
XLA Modules:
  0.0 1650.5 jit_solution(8481411095860062708)
XLA Ops:
  11.8 7.2 all-reduce.10
  19.3 21.2 %all-gather.12.cloned.1.call-done = bf16[768,768]{1,0:T(8,128)(2,1)} async-done(((bf16[192,768]{1,0:T(8,128)(2,1)}), bf16[768,768]{1,0:T(8,128)(2,1)}) %all-gather.12.cloned.1.call-update) | async-done | bytes 1179664 | tf_op jit(solution)/shard_map/all_gather | solution.py:129
  43.6 28.1 %all-gather.18.cloned.1.call-done = bf16[768,768]{1,0:T(8,128)(2,1)} async-done(((bf16[192,768]{1,0:T(8,128)(2,1)}), bf16[768,768]{1,0:T(8,128)(2,1)}) %all-gather.18.cloned.1.call-update) | async-done | bytes 1179664 | tf_op jit(solution)/shard_map/all_gather | solution.py:130
  77.1 8.5 all_gather.64
  86.8 16.1 all-gather.16.cloned.1.call-done
  106.5 84.5 %all-gather.28.cloned.1.call-done = bf16[3072,768]{1,0:T(8,128)(2,1)} async-done(((bf16[768,768]{1,0:T(8,128)(2,1)}), bf16[3072,768]{1,0:T(8,128)(2,1)}) %all-gather.28.cloned.1.call-update) | async-done | bytes 4718608 | tf_op jit(solution)/shard_map/all_gather | solution.py:136
  191.1 6.9 fusion.42
  197.9 42.5 %all-gather.14.cloned.1.call-done = bf16[4,1024,768]{2,1,0:T(8,128)(2,1)} async-done(((bf16[4,128,768]{2,1,0:T(8,128)(2,1)}), bf16[4,1024,768]{2,1,0:T(8,128)(2,1)}) %all-gather.14.cloned.1.call-update) | async-done | bytes 6291472 | tf_op jit(solution)/shard_map/all_gather | solution.py:221
  240.4 8.7 copy.112
  249.1 38.7 %all-gather.20.cloned.1.call-done = bf16[4,1024,768]{2,1,0:T(8,128)(2,1)} async-done(((bf16[4,128,768]{2,1,0:T(8,128)(2,1)}), bf16[4,1024,768]{2,1,0:T(8,128)(2,1)}) %all-gather.20.cloned.1.call-update) | async-done | bytes 6291472 | tf_op jit(solution)/shard_map/all_gather | solution.py:222
  287.8 8.7 copy.113
  296.5 94.9 %while.62 = (s32[]{:T(128)}, f32[4,12,128]{2,1,0:T(8,128)S(1)}, f32[4,12,128]{2,1,0:T(8,128)S(1)}, f32[4,128,12,64]{1,3,2,0:T(8,128)}, s32[4]{0:T(128)S(1)}, /*i...) while((s32[]{:T(128)}, f32[4,12,128]{2,1,0:T(8,128)S(1)}, ...), condition=%wide.region_4.5_spmd.clone, body=%wide.region_1.4_spmd.clone.sunk | while | flops 421181696 | bytes 90909992 | solution.py:95
  311.9 6.0 bitcast_add_fusion.10
  335.6 6.5 bitcast_add_fusion.10
  359.3 6.4 bitcast_add_fusion.10
  383.1 6.4 bitcast_add_fusion.10
  395.9 11.0 all-gather.26.cloned.1.call-done
  406.9 7.2 fusion.48
  414.1 82.3 %all-gather.24.cloned.1.call-done = bf16[768,3072]{1,0:T(8,128)(2,1)} async-done(((bf16[192,3072]{1,0:T(8,128)(2,1)}), bf16[768,3072]{1,0:T(8,128)(2,1)}) %all-gather.24.cloned.1.call-update) | async-done | bytes 4718608 | tf_op jit(solution)/shard_map/all_gather | solution.py:134
  496.4 14.2 fusion.39
  531.5 151.5 %while.63 = (s32[]{:T(128)}, f32[4,128,12,64]{1,3,2,0:T(8,128)}, f32[12,2047]{1,0:T(8,128)S(1)}, bf16[4,1024,768]{1,2,0:T(8,128)(2,1)}, s32[4]{0:T(128)S(1)}, /*...) while((s32[]{:T(128)}, f32[4,128,12,64]{1,3,2,0:T(8,128)}, ...), condition=%wide.region_10.11_spmd.clone, body=%wide.region_7.10_spmd.clone.sunk | while | flops 617560832 | bytes 110347248 | solution.py:95
  546.4 5.4 convert_reduce_fusion.2
  558.0 4.3 reshape.398
  583.9 5.4 convert_reduce_fusion.2
  595.4 4.3 reshape.398
  603.5 3.8 bitcast_add_fusion.11
  622.1 5.5 convert_reduce_fusion.2
  633.7 4.3 reshape.398
  641.4 3.8 bitcast_add_fusion.11
  659.9 5.4 convert_reduce_fusion.2
  671.5 4.3 reshape.398
  679.2 3.8 bitcast_add_fusion.11
  685.2 10.8 all_gather.75
  696.0 10.8 all_gather.73
  709.3 182.8 %while.64 = (s32[]{:T(128)}, f32[4,128,12,64]{1,3,2,0:T(8,128)}, f32[4,128,12,64]{1,3,2,0:T(8,128)}, bf16[4,1024,768]{2,1,0:T(8,128)(2,1)}, bf16[4,128,12,64]{1,...) while((s32[]{:T(128)}, f32[4,128,12,64]{1,3,2,0:T(8,128)}, ...), condition=%wide.region_12.0_spmd.clone, body=%wide.region_11.12_spmd.clone.sunk | while | flops 822617600 | bytes 99482848 | solution.py:95
  712.3 3.6 copy.181
  718.9 8.4 reshape.399
  733.7 5.2 fusion.180
  742.2 5.0 bitcast_add_fusion.13
  747.2 7.9 bitcast_add_fusion.12
  764.3 8.4 reshape.399
  779.0 5.2 fusion.180
  787.5 5.2 bitcast_add_fusion.13
  792.7 8.0 bitcast_add_fusion.12
  809.9 8.4 reshape.399
  824.6 5.2 fusion.180
  833.1 5.2 bitcast_add_fusion.13
  838.4 8.0 bitcast_add_fusion.12
  855.5 8.4 reshape.399
  870.2 5.2 fusion.180
  878.8 5.2 bitcast_add_fusion.13
  884.0 8.0 bitcast_add_fusion.12
  902.1 7.4 convolution_bitcast_fusion.2
  909.6 7.0 convolution_bitcast_fusion.1
  917.7 8.3 convolution_bitcast_fusion
  926.3 16.0 reduce-scatter.10.cloned.1.call-done
  942.4 50.3 %reduce-scatter.12.cloned.1.call-done = f32[192,768]{1,0:T(8,128)} async-done(((f32[768,768]{1,0:T(8,128)}), f32[192,768]{1,0:T(8,128)}) %reduce-scatter.12.cloned.1.call-update) | async-done | bytes 589840 | tf_op jit(solution)/shard_map/reduce_scatter | solution.py:408
  992.7 165.2 %reduce-scatter.16.cloned.1.call-done = f32[192,3072]{1,0:T(8,128)} async-done(((f32[768,3072]{1,0:T(8,128)}), f32[192,3072]{1,0:T(8,128)}) %reduce-scatter.16.cloned.1.call-update) | async-done | bytes 2359312 | tf_op jit(solution)/shard_map/reduce_scatter | solution.py:412
  1157.9 164.4 %reduce-scatter.18.cloned.1.call-done = f32[192,3072]{1,0:T(8,128)} async-done(((f32[768,3072]{1,0:T(8,128)}), f32[192,3072]{1,0:T(8,128)}) %reduce-scatter.18.cloned.1.call-update) | async-done | bytes 2359312 | tf_op jit(solution)/shard_map/reduce_scatter | solution.py:413
  1322.2 164.4 %reduce-scatter.20.cloned.1.call-done = f32[768,768]{1,0:T(8,128)} async-done(((f32[3072,768]{1,0:T(8,128)}), f32[768,768]{1,0:T(8,128)}) %reduce-scatter.20.cloned.1.call-update) | async-done | bytes 2359312 | tf_op jit(solution)/shard_map/reduce_scatter | solution.py:414
  1491.3 6.9 multiply_convert_fusion.6
  1502.2 12.5 all-reduce.9
  1514.9 15.7 all-reduce.7
  1533.7 99.1 %all-reduce.13.cloned.1.call-done = (f32[192,768]{1,0:T(8,128)}, f32[192,768]{1,0:T(8,128)}, f32[192,768]{1,0:T(8,128)}, f32[192,768]{1,0:T(8,128)}, f32[192,307...) async-done(((f32[192,768]{1,0:T(8,128)}, f32[192,768]{1,0:T(8,128)}, f32[192,768]{1,0:T(8,128)}, f32[192,768]{1,0:T(8,128)}, f32[192,3072]{1,0:T(8,128)}, ...) | async-done | bytes 9437200 | tf_op jit(solution)/shard_map/psum | solution.py:416
  (503 shorter events, 320.9 us)
Async XLA Ops:
  7.2 2.9 copy-start.52
  7.2 4.2 copy-start.58
  7.2 4.4 copy-start.59
  7.2 11.9 copy-start.6
  7.2 33.4 %all-gather.12.cloned.1.call-start = ((), (), s32[]{:S(2)}) async-start(), calls=%async_computation.7 | async-start | bytes 1474560 | tf_op jit(solution)/shard_map/all_gather | solution.py:129
  8.0 63.8 %all-gather.18.cloned.1.call-start = ((), (), s32[]{:S(2)}) async-start(), calls=%async_computation.10 | async-start | bytes 1474560 | tf_op jit(solution)/shard_map/all_gather | solution.py:130
  8.7 94.3 %all-gather.16.cloned.1.call-start = ((), (), s32[]{:S(2)}) async-start(), calls=%async_computation.9 | async-start | bytes 1474560 | tf_op jit(solution)/shard_map/all_gather | solution.py:128
  9.4 181.6 %all-gather.28.cloned.1.call-start = ((), (), s32[]{:S(2)}) async-start(), calls=%async_computation.15 | async-start | bytes 5898240 | tf_op jit(solution)/shard_map/all_gather | solution.py:136
  10.0 230.4 %all-gather.14.cloned.1.call-start = ((), (), s32[]{:S(2)}) async-start(), calls=%async_computation.8 | async-start | bytes 7077888 | tf_op jit(solution)/shard_map/all_gather | solution.py:221
  19.1 83.9 %copy-start.41 = (f32[768]{0:T(1024)}, f32[768]{0:T(1024)S(1)}, u32[]{:S(2)}) copy-start(f32[768]{0:T(1024)S(1)} %convert_element_type.161) | copy-start | bytes 9220
  19.3 24.3 %copy-start.46 = (f32[4,128]{1,0:T(4,128)}, f32[4,128]{1,0:T(4,128)S(1)}, u32[]{:S(2)}) copy-start(f32[4,128]{1,0:T(4,128)S(1)} %fusion.60) | copy-start | bytes 6148
  19.3 83.6 %copy-start.43 = (f32[4,128]{1,0:T(4,128)}, f32[4,128]{1,0:T(4,128)S(1)}, u32[]{:S(2)}) copy-start(f32[4,128]{1,0:T(4,128)S(1)} %fusion.89) | copy-start | bytes 6148
  43.6 244.2 %all-gather.20.cloned.1.call-start = ((), (), s32[]{:S(2)}) async-start(), calls=%async_computation.11 | async-start | bytes 7077888 | tf_op jit(solution)/shard_map/all_gather | solution.py:222
  74.7 10.9 copy-start.45
  74.7 10.9 copy-start.56
  74.8 318.4 %all-gather.22.cloned.1.call-start = ((), (), s32[]{:S(2)}) async-start(), calls=%async_computation.12 | async-start | bytes 1474560 | tf_op jit(solution)/shard_map/all_gather | solution.py:131
  75.5 331.4 %all-gather.26.cloned.1.call-start = ((), (), s32[]{:S(2)}) async-start(), calls=%async_computation.14 | async-start | bytes 5898240 | tf_op jit(solution)/shard_map/all_gather | solution.py:135
  76.3 420.1 %all-gather.24.cloned.1.call-start = ((), (), s32[]{:S(2)}) async-start(), calls=%async_computation.13 | async-start | bytes 5898240 | tf_op jit(solution)/shard_map/all_gather | solution.py:134
  77.0 632.3 %all-gather.30.cloned.1.call-start = ((), (), s32[]{:S(2)}) async-start(), calls=%async_computation.16 | async-start | bytes 7077888 | tf_op jit(solution)/shard_map/all_gather | solution.py:372
  85.6 19.5 %copy-start.53 = (s32[128]{0:T(128)}, s32[128]{0:T(128)S(1)}, u32[]{:S(2)}) copy-start(s32[128]{0:T(128)S(1)} %iota_add_fusion.2) | copy-start | bytes 1540
  85.7 433.0 %copy-start.48 = (f32[4,128]{1,0:T(4,128)}, f32[4,128]{1,0:T(4,128)S(1)}, u32[]{:S(2)}) copy-start(f32[4,128]{1,0:T(4,128)S(1)} %compare_convert_fusion) | copy-start | bytes 6148
  105.1 86.0 %copy-start.33 = (bf16[4,128,768]{2,1,0:T(8,128)(2,1)S(1)}, bf16[4,128,768]{2,1,0:T(8,128)(2,1)}, u32[]{:S(2)}) copy-start(bf16[4,128,768]{2,1,0:T(8,128)(2,1)} %param.21) | copy-start | bytes 2359300
  106.3 603.0 %all-gather.32.cloned.1.call-start = ((), (), s32[]{:S(2)}) async-start(), calls=%async_computation.17 | async-start | bytes 7077888 | tf_op jit(solution)/shard_map/all_gather | solution.py:373
  311.9 6.0 slice-start
  311.9 6.0 slice-start.1
  329.4 2.5 copy-start.2
  335.5 6.5 slice-start
  335.6 6.5 slice-start.1
  359.3 6.4 slice-start
  359.3 6.4 slice-start.1
  383.1 6.4 slice-start
  383.1 6.4 slice-start.1
  393.1 2.5 copy-start.16
  395.6 117.6 %copy-start.12 = (f32[4,128,768]{2,1,0:T(8,128)}, f32[4,128,768]{2,1,0:T(8,128)S(1)}, u32[]{:S(2)}) copy-start(f32[4,128,768]{2,1,0:T(8,128)S(1)} %get-tuple-element.1458) | copy-start | bytes 4718596
  395.8 100.5 %copy-start.14 = (bf16[4,128,768]{2,1,0:T(8,128)(2,1)}, bf16[4,128,768]{2,1,0:T(8,128)(2,1)S(1)}, u32[]{:S(2)}) copy-start(bf16[4,128,768]{2,1,0:T(8,128)(2,1)S(1)} %multiply_convert_fusion.7) | copy-start | bytes 2359300
  496.4 14.2 copy-start.17
  510.6 2.7 copy-start.22
  510.6 3.2 copy-start.23
  510.6 4.6 copy-start.54
  515.2 3.5 copy-start.34
  520.8 5.5 copy-start.10
  522.5 403.8 %reduce-scatter.14.cloned.1.call-start = ((), (), s32[]{:S(2)}) async-start(), calls=%async_computation.21 | async-start | bytes 2949120 | tf_op jit(solution)/shard_map/reduce_scatter | solution.py:409
  526.3 3.4 copy-start.4
  531.2 395.1 %reduce-scatter.8.cloned.1.call-start = ((), (), s32[]{:S(2)}) async-start(), calls=%async_computation.18 | async-start | bytes 2949120 | tf_op jit(solution)/shard_map/reduce_scatter | solution.py:406
  683.0 23.8 %copy-start.8 = (bf16[4,128,768]{2,1,0:T(8,128)(2,1)S(1)}, bf16[4,128,768]{2,1,0:T(8,128)(2,1)}, u32[]{:S(2)}) copy-start(bf16[4,128,768]{2,1,0:T(8,128)(2,1)} %param.20) | copy-start | bytes 2359300
  683.0 23.9 %copy-start.42 = (f32[768]{0:T(1024)S(1)}, f32[768]{0:T(1024)}, u32[]{:S(2)}) copy-start(f32[768]{0:T(1024)} %copy-done.41) | copy-start | bytes 9220
  683.0 23.9 %copy-start.44 = (f32[4,128]{1,0:T(4,128)S(1)}, f32[4,128]{1,0:T(4,128)}, u32[]{:S(2)}) copy-start(f32[4,128]{1,0:T(4,128)} %copy-done.43) | copy-start | bytes 6148
  685.2 21.6 %copy-start.24 = (bf16[4,128,12,64]{1,3,2,0:T(8,128)(2,1)}, bf16[4,128,12,64]{1,3,2,0:T(8,128)(2,1)S(1)}, u32[]{:S(2)}) copy-start(bf16[4,128,12,64]{1,3,2,0:T(8,128)(2,1)S(1)} %convert_element_type.178) | copy-start | bytes 2359300
  709.2 233.1 %reduce-scatter.10.cloned.1.call-start = ((), (), s32[]{:S(2)}) async-start(), calls=%async_computation.19 | async-start | bytes 2949120 | tf_op jit(solution)/shard_map/reduce_scatter | solution.py:407
  892.2 2.5 copy-start.9
  897.1 95.6 %reduce-scatter.12.cloned.1.call-start = ((), (), s32[]{:S(2)}) async-start(), calls=%async_computation.20 | async-start | bytes 2949120 | tf_op jit(solution)/shard_map/reduce_scatter | solution.py:408
  901.0 256.9 %reduce-scatter.16.cloned.1.call-start = ((), (), s32[]{:S(2)}) async-start(), calls=%async_computation.22 | async-start | bytes 11796480 | tf_op jit(solution)/shard_map/reduce_scatter | solution.py:412
  909.6 412.7 %reduce-scatter.18.cloned.1.call-start = ((), (), s32[]{:S(2)}) async-start(), calls=%async_computation.23 | async-start | bytes 11796480 | tf_op jit(solution)/shard_map/reduce_scatter | solution.py:413
  916.6 570.0 %reduce-scatter.20.cloned.1.call-start = ((), (), s32[]{:S(2)}) async-start(), calls=%async_computation.24 | async-start | bytes 11796480 | tf_op jit(solution)/shard_map/reduce_scatter | solution.py:414
  926.0 706.7 %all-reduce.13.cloned.1.call-start = ((), (), s32[]{:S(2)}) async-start(), calls=%async_computation.25 | async-start | bytes 18874368 | tf_op jit(solution)/shard_map/psum | solution.py:416
  1491.3 6.9 copy-start.27
  1491.3 6.9 copy-start.55
  1499.9 30.8 %copy-start.47 = (f32[4,128]{1,0:T(4,128)S(1)}, f32[4,128]{1,0:T(4,128)}, u32[]{:S(2)}) copy-start(f32[4,128]{1,0:T(4,128)} %copy-done.46) | copy-start | bytes 6148
  1499.9 30.8 %copy-start.11 = (f32[4,128,768]{2,1,0:T(8,128)S(1)}, f32[4,128,768]{2,1,0:T(8,128)}, u32[]{:S(2)}) copy-start(f32[4,128,768]{2,1,0:T(8,128)} %copy-done.10) | copy-start | bytes 4718596
  1632.8 2.9 copy-start.37
  1632.8 3.7 copy-start.36
  1634.8 2.5 copy-start.30
  1637.3 2.5 copy-start.29
  1639.8 2.5 copy-start.28
  (43 other events, 71.4 us)
Sparse Core Ops, SparseCore 0:
  9.6 30.9 all-gather.11
  42.1 29.5 all-gather.17
  73.3 29.5 all-gather.15
  104.4 86.6 all-gather.27
  193.4 46.9 all-gather.13
  242.2 45.5 all-gather.19
  289.3 29.2 all-gather.21
  320.2 86.6 all-gather.25
  408.5 87.8 all-gather.23
  498.1 46.9 all-gather.29
  547.1 45.5 all-gather.31
  594.8 45.2 reduce-scatter.13
  709.4 45.1 reduce-scatter.7
  897.2 45.1 reduce-scatter.9
  945.1 47.5 reduce-scatter.11
  994.9 162.9 reduce-scatter.15
  1160.1 162.1 reduce-scatter.17
  1324.5 162.1 reduce-scatter.19
  1491.4 141.3 all-reduce.12
where the time goes:
time: 1660 us; the launch traced here: 1650 us
  waiting for transfers between devices  989 us (60%)
  local copies, waits for them, and re-layouts  303 us (18%)
  matrix products  248 us (15%)
  blocking collectives  65.6 us (4%)
  other arithmetic  24.9 us (2%)
  between operations  16.9 us (1%)
    reduce_scatter x1, waiting for transfers between devices, per_device(): lax.psum_scatter(grads[7], 'fsdp', scatter_dimension=0, tiled=True)  165 us
    reduce_scatter x1, waiting for transfers between devices, per_device(): lax.psum_scatter(grads[9], 'fsdp', scatter_dimension=0, tiled=True)  164 us
    reduce_scatter x1, waiting for transfers between devices, per_device(): lax.psum_scatter(grads[8], 'fsdp', scatter_dimension=0, tiled=True)  164 us
    psum x1, waiting for transfers between devices, per_device(): lax.psum((shard_sums[0], shard_sums[1], shard_sums[2], shard_sums[3], sha...  99.1 us
    all_gather x1, waiting for transfers between devices, per_device(): lax.all_gather(shards[9], 'fsdp', axis=0, tiled=True)  84.5 us
    all_gather x1, waiting for transfers between devices, per_device(): lax.all_gather(shards[7], 'fsdp', axis=0, tiled=True)  82.3 us
    reshape x12, local copies, waits for them, and re-layouts, toeplitz_bias(): tiled[:, :query_rows * span].reshape(window.shape[0], query_rows, span)  60.6 us
    while x84, local copies, waits for them, and re-layouts  51.7 us
  transfers between devices with their start and end apart: 19, of which 14 were waited for; matrix products, arithmetic and copies ran while one was open for 33% of the time, Pallas kernels for 0%

commit v1 on v0

--- a/solution.py
+++ b/solution.py
@@ -1,16 +1,878 @@
+import functools
 import math
 
 import jax
 import jax.numpy as jnp
 from jax import lax
+from jax.experimental import pallas as pl
+from jax.experimental.pallas import tpu as pltpu
 from jax.sharding import PartitionSpec as P
 
 HEADS = 12
 HEAD_DIM = 64
 BUCKETS = 32
-
+BLOCK = 256
+VMEM_BYTES = 56 * 1024 * 1024
+TILE = 256
 
 norm_eps = 1e-06
+F32 = jnp.float32
+LOW = jnp.bfloat16
+NT = (((1,), (1,)), ((), ()))
+NN = (((1,), (0,)), ((), ()))
+TN = (((0,), (0,)), ((), ()))
+
+
+def dot(left, right, dims=NN):
+    return lax.dot_general(left, right, dims, preferred_element_type=F32)
+
+
+def block_rows(index, rows=BLOCK):
+    return pl.ds(pl.multiple_of(index * rows, rows), rows)
+
+
+def build_bias(offsets_ref, bias_ref):
+    heads, _, width = bias_ref.shape
+    span = offsets_ref.shape[1]
+    for head in range(heads):
+        line = jnp.broadcast_to(offsets_ref[head : head + 1, :], (8, span))
+        for group in range(BLOCK // 8):
+            turned = pltpu.roll(
+                line, (group * 8 - (BLOCK - 1)) % span, 1, stride=1, stride_axis=0
+            )
+            bias_ref[head, group * 8 : group * 8 + 8, :] = turned[:, :width]
+
+
+def fold_diagonals(bias_grad_ref, offsets_grad_ref):
+    heads, _, width = bias_grad_ref.shape
+    span = offsets_grad_ref.shape[1]
+    for head in range(heads):
+        total = jnp.zeros((8, span), F32)
+        for group in range(BLOCK // 8):
+            rows = bias_grad_ref[head, group * 8 : group * 8 + 8, :]
+            wide = jnp.concatenate([rows, jnp.zeros((8, span - width), F32)], axis=1)
+            total = total + pltpu.roll(wide, (BLOCK - 8 - group * 8) % span, 1)
+        line = jnp.zeros((1, span), F32)
+        for row in range(8):
+            line = line + pltpu.roll(total, (7 - row) % span, 1)[row : row + 1, :]
+        offsets_grad_ref[head : head + 1, :] = line
+
+
+def rms_rows(rows_f):
+    return lax.rsqrt(jnp.mean(rows_f * rows_f, axis=-1, keepdims=True) + norm_eps)
+
+
+def attn_forward_kernel(
+    lens_ref, tok_ref, gain_ref, w_ref, off_ref,
+    o_ref, of_ref, lse_ref, q_ref, k_ref, v_ref,
+    bias_ref, vm_ref,
+):
+    slot = pl.program_id(0)
+    blocks = tok_ref.shape[1] // BLOCK
+    per_chip, width = w_ref.shape[2] // HEAD_DIM, w_ref.shape[2]
+    length = lens_ref[slot]
+    used = (length + BLOCK - 1) // BLOCK
+
+    @pl.when(slot == 0)
+    def _():
+        build_bias(off_ref, bias_ref)
+
+    owner = lax.broadcasted_iota(jnp.int32, (BLOCK, width), 1) // HEAD_DIM
+    column = lax.broadcasted_iota(jnp.int32, (BLOCK, BLOCK), 1)
+    nothing = jnp.zeros((BLOCK, width), LOW)
+    parts = BLOCK // o_ref.shape[2]
+
+    def project(index, carry):
+        rows = block_rows(index)
+        rows_f = tok_ref[0, rows, :].astype(F32)
+        normed = (rows_f * rms_rows(rows_f) * gain_ref[...]).astype(LOW)
+        q_ref[0, rows, :] = dot(normed, w_ref[0]).astype(LOW)
+        k_ref[0, rows, :] = dot(normed, w_ref[1]).astype(LOW)
+        val = dot(normed, w_ref[2]).astype(LOW)
+        v_ref[0, rows, :] = val
+        for head in range(per_chip):
+            vm_ref[head, rows, :] = jnp.where(owner == head, val, nothing)
+        return carry
+
+    lax.fori_loop(0, used, project, 0)
+
+    def attend(index, carry):
+        rows = block_rows(index)
+        query = q_ref[0, rows, :]
+        start = pl.multiple_of((blocks - 1 - index) * BLOCK, BLOCK)
+        for count in range(1, blocks + 1):
+
+            @pl.when(used == count)
+            def _(count=count):
+                wide = count * BLOCK
+                total = jnp.zeros((BLOCK, width), F32)
+                for head in range(per_chip):
+                    mine = jnp.where(owner == head, query, nothing)
+                    scores = dot(mine, k_ref[0, :wide, :], NT)
+                    scores = scores + bias_ref[head, :, pl.ds(start, wide)]
+                    tail = jnp.where(
+                        column < length - (count - 1) * BLOCK, scores[:, wide - BLOCK :], -1e30
+                    )
+                    if count > 1:
+                        scores = jnp.concatenate([scores[:, : wide - BLOCK], tail], axis=1)
+                    else:
+                        scores = tail
+                    top = jnp.max(scores, axis=-1, keepdims=True)
+                    weights = jnp.exp(scores - top)
+                    row_total = jnp.sum(weights, axis=-1, keepdims=True)
+                    probs = (weights * (1.0 / row_total)).astype(LOW)
+                    total = total + dot(probs, vm_ref[head, :wide, :])
+                    lse_ref[0, head, rows, :] = jnp.broadcast_to(
+                        top + jnp.log(row_total), (BLOCK, 128)
+                    )
+                of_ref[0, rows, :] = total
+                o_ref[pl.ds(index * parts, parts), 0] = total.astype(LOW).reshape(
+                    parts, BLOCK // parts, width
+                )
+
+        return carry
+
+    lax.fori_loop(0, used, attend, 0)
+
+    def clear(index, carry):
+        o_ref[pl.ds(index * parts, parts), 0] = jnp.zeros((parts, BLOCK // parts, width), LOW)
+        return carry
+
+    lax.fori_loop(used, blocks, clear, 0)
+
+
+def attn_forward(lens, tokens, gain, w_qkv, offsets, pieces):
+    slots, seq, model = tokens.shape
+    width = w_qkv.shape[2]
+    per_chip = width // HEAD_DIM
+    rows = seq // pieces
+    lane_rows = pl.BlockSpec((1, seq, width), lambda s: (s, 0, 0))
+    return pl.pallas_call(
+        attn_forward_kernel,
+        grid=(slots,),
+        in_specs=[
+            pl.BlockSpec(memory_space=pltpu.SMEM),
+            pl.BlockSpec((1, seq, model), lambda s: (s, 0, 0)),
+            pl.BlockSpec((1, model), lambda s: (0, 0)),
+            pl.BlockSpec((3, model, width), lambda s: (0, 0, 0)),
+            pl.BlockSpec(offsets.shape, lambda s: (0, 0)),
+        ],
+        out_specs=[
+            pl.BlockSpec((pieces, 1, rows, width), lambda s: (0, s, 0, 0)),
+            lane_rows,
+            pl.BlockSpec((1, per_chip, seq, 128), lambda s: (s, 0, 0, 0)),
+            lane_rows,
+            lane_rows,
+            lane_rows,
+        ],
+        out_shape=[
+            jax.ShapeDtypeStruct((pieces, slots, rows, width), LOW),
+            jax.ShapeDtypeStruct((slots, seq, width), F32),
+            jax.ShapeDtypeStruct((slots, per_chip, seq, 128), F32),
+            jax.ShapeDtypeStruct((slots, seq, width), LOW),
+            jax.ShapeDtypeStruct((slots, seq, width), LOW),
+            jax.ShapeDtypeStruct((slots, seq, width), LOW),
+        ],
+        scratch_shapes=[
+            pltpu.VMEM((per_chip, BLOCK, 2 * seq - BLOCK), F32),
+            pltpu.VMEM((per_chip, seq, width), LOW),
+        ],
+        compiler_params=pltpu.CompilerParams(vmem_limit_bytes=VMEM_BYTES),
+        cost_estimate=pl.CostEstimate(
+            flops=2 * slots * seq * (model * 3 * width + 2 * seq * 256 * per_chip),
+            bytes_accessed=slots * seq * 2 * (model + 8 * width),
+            transcendentals=slots * seq * seq * per_chip,
+        ),
+        name="attn_forward",
+    )(lens, tokens, gain, w_qkv, offsets)
+
+
+def attn_backward_kernel(
+    lens_ref, tok_ref, gain_ref, w_ref, off_ref, q_ref, k_ref, v_ref, of_ref, lse_ref, do_ref,
+    dn_ref, dw_ref, dgain_ref, doff_ref,
+    bias_ref, dbias_ref, km_ref, dq_ref, dqt_ref, dkt_ref, dvt_ref,
+):
+    slot = pl.program_id(0)
+    blocks = tok_ref.shape[1] // BLOCK
+    per_chip, width = w_ref.shape[2] // HEAD_DIM, w_ref.shape[2]
+    length = lens_ref[slot]
+    used = (length + BLOCK - 1) // BLOCK
+    parts = BLOCK // do_ref.shape[2]
+
+    @pl.when(slot == 0)
+    def _():
+        build_bias(off_ref, bias_ref)
+        dbias_ref[...] = jnp.zeros_like(dbias_ref)
+        dw_ref[...] = jnp.zeros_like(dw_ref)
+        dgain_ref[...] = jnp.zeros_like(dgain_ref)
+
+    dkt_ref[...] = jnp.zeros_like(dkt_ref)
+    dvt_ref[...] = jnp.zeros_like(dvt_ref)
+    owner = lax.broadcasted_iota(jnp.int32, (BLOCK, width), 1) // HEAD_DIM
+    column = lax.broadcasted_iota(jnp.int32, (BLOCK, BLOCK), 1)
+    nothing = jnp.zeros((BLOCK, width), LOW)
+
+    def split_keys(index, carry):
+        rows = block_rows(index)
+        key = k_ref[0, rows, :]
+        for head in range(per_chip):
+            km_ref[head, rows, :] = jnp.where(owner == head, key, nothing)
+        return carry
+
+    lax.fori_loop(0, used, split_keys, 0)
+
+    def attend(index, carry):
+        rows = block_rows(index)
+        query = q_ref[0, rows, :]
+        grad = do_ref[pl.ds(index * parts, parts), 0].reshape(BLOCK, width)
+        query_t = jnp.transpose(query)
+        grad_t = jnp.transpose(grad)
+        product = grad.astype(F32) * of_ref[0, rows, :]
+        start = pl.multiple_of((blocks - 1 - index) * BLOCK, BLOCK)
+        for count in range(1, blocks + 1):
+
+            @pl.when(used == count)
+            def _(count=count):
+                wide = count * BLOCK
+                grad_query = jnp.zeros((BLOCK, width), F32)
+                for head in range(per_chip):
+                    lanes = slice(head * HEAD_DIM, (head + 1) * HEAD_DIM)
+                    mine = jnp.where(owner == head, query, nothing)
+                    scores = dot(mine, k_ref[0, :wide, :], NT)
+                    scores = scores + bias_ref[head, :, pl.ds(start, wide)]
+                    tail = jnp.where(
+                        column < length - (count - 1) * BLOCK, scores[:, wide - BLOCK :], -1e30
+                    )
+                    if count > 1:
+                        scores = jnp.concatenate([scores[:, : wide - BLOCK], tail], axis=1)
+                    else:
+                        scores = tail
+                    probs = jnp.exp(scores - lse_ref[0, head, rows, :][:, :1])
+                    delta = jnp.sum(
+                        jnp.where(owner == head, product, 0.0), axis=-1, keepdims=True
+                    )
+                    grad_mine = jnp.where(owner == head, grad, nothing)
+                    grad_probs = dot(grad_mine, v_ref[0, :wide, :], NT)
+                    grad_scores = (probs * (grad_probs - delta)).astype(LOW)
+                    grad_query = grad_query + dot(grad_scores, km_ref[head, :wide, :])
+                    dkt_ref[lanes, :wide] += dot(query_t[lanes, :], grad_scores)
+                    dvt_ref[lanes, :wide] += dot(grad_t[lanes, :], probs.astype(LOW))
+                    dbias_ref[head, :, pl.ds(start, wide)] += grad_scores.astype(F32)
+                dq_ref[rows, :] = grad_query.astype(LOW)
+
+        return carry
+
+    lax.fori_loop(0, used, attend, 0)
+
+    def finish(index, carry):
+        rows = block_rows(index)
+        grad_query = dq_ref[rows, :]
+        key_t = dkt_ref[:, rows].astype(LOW)
+        value_t = dvt_ref[:, rows].astype(LOW)
+        rows_f = tok_ref[0, rows, :].astype(F32)
+        unit = rows_f * rms_rows(rows_f)
+        normed = (unit * gain_ref[...]).astype(LOW)
+        grad_normed = (
+            dot(grad_query, w_ref[0], NT)
+            + dot(jnp.transpose(key_t), w_ref[1], NT)
+            + dot(jnp.transpose(value_t), w_ref[2], NT)
+        )
+        dgain_ref[...] += jnp.sum(grad_normed * unit, axis=0, keepdims=True)
+        dn_ref[index, 0] = grad_normed.astype(LOW)
+        dw_ref[0:width, :] += dot(jnp.transpose(grad_query), normed)
+        dw_ref[width : 2 * width, :] += dot(key_t, normed)
+        dw_ref[2 * width :, :] += dot(value_t, normed)
+        return carry
+
+    lax.fori_loop(0, used, finish, 0)
+
+    def clear(index, carry):
+        dn_ref[index, 0] = jnp.zeros(dn_ref.shape[2:], LOW)
+        return carry
+
+    lax.fori_loop(used, blocks, clear, 0)
+
+    @pl.when(slot == pl.num_programs(0) - 1)
+    def _():
+        fold_diagonals(dbias_ref, doff_ref)
+
+
+def attn_backward(lens, tokens, gain, w_qkv, offsets, query, key, value, attn_full, lse, grad):
+    slots, seq, model = tokens.shape
+    width = w_qkv.shape[2]
+    per_chip = width // HEAD_DIM
+    pieces, _, rows, _ = grad.shape
+    blocks = seq // BLOCK
+    lane_rows = pl.BlockSpec((1, seq, width), lambda s: (s, 0, 0))
+    return pl.pallas_call(
+        attn_backward_kernel,
+        grid=(slots,),
+        in_specs=[
+            pl.BlockSpec(memory_space=pltpu.SMEM),
+            pl.BlockSpec((1, seq, model), lambda s: (s, 0, 0)),
+            pl.BlockSpec((1, model), lambda s: (0, 0)),
+            pl.BlockSpec((3, model, width), lambda s: (0, 0, 0)),
+            pl.BlockSpec(offsets.shape, lambda s: (0, 0)),
+            lane_rows,
+            lane_rows,
+            lane_rows,
+            lane_rows,
+            pl.BlockSpec((1, per_chip, seq, 128), lambda s: (s, 0, 0, 0)),
+            pl.BlockSpec((pieces, 1, rows, width), lambda s: (0, s, 0, 0)),
+        ],
+        out_specs=[
+            pl.BlockSpec((blocks, 1, BLOCK, model), lambda s: (0, s, 0, 0)),
+            pl.BlockSpec((3 * width, model), lambda s: (0, 0)),
+            pl.BlockSpec((1, model), lambda s: (0, 0)),
+            pl.BlockSpec(offsets.shape, lambda s: (0, 0)),
+        ],
+        out_shape=[
+            jax.ShapeDtypeStruct((blocks, slots, BLOCK, model), LOW),
+            jax.ShapeDtypeStruct((3 * width, model), F32),
+            jax.ShapeDtypeStruct((1, model), F32),
+            jax.ShapeDtypeStruct(offsets.shape, F32),
+        ],
+        scratch_shapes=[
+            pltpu.VMEM((per_chip, BLOCK, 2 * seq - BLOCK), F32),
+            pltpu.VMEM((per_chip, BLOCK, 2 * seq - BLOCK), F32),
+            pltpu.VMEM((per_chip, seq, width), LOW),
+            pltpu.VMEM((seq, width), LOW),
+            pltpu.VMEM((width, BLOCK), LOW),
+            pltpu.VMEM((width, seq), F32),
+            pltpu.VMEM((width, seq), F32),
+        ],
+        compiler_params=pltpu.CompilerParams(vmem_limit_bytes=VMEM_BYTES),
+        cost_estimate=pl.CostEstimate(
+            flops=2 * slots * seq * (model * 6 * width + 5 * seq * 256 * per_chip),
+            bytes_accessed=slots * seq * 2 * (2 * model + 12 * width),
+            transcendentals=slots * seq * seq * per_chip,
+        ),
+        name="attn_backward",
+    )(lens, tokens, gain, w_qkv, offsets, query, key, value, attn_full, lse, grad)
+
+
+def out_project_kernel(tok_ref, attn_ref, w_ref, gain_ref, res_ref, nf_ref):
+    chips = attn_ref.shape[0] // 2
+    width = attn_ref.shape[3]
+    rows = tok_ref.shape[0]
+    total = tok_ref[...].astype(F32)
+    for chip in range(chips):
+        part = attn_ref[2 * chip : 2 * chip + 2].reshape(rows, width)
+        total = total + dot(part, w_ref[chip * width : (chip + 1) * width, :])
+    res_ref[...] = total
+    nf_ref[...] = (total * rms_rows(total) * gain_ref[...]).astype(LOW)
+
+
+def out_project(tokens, attn, w_out, gain):
+    rows, model = tokens.shape
+    return pl.pallas_call(
+        out_project_kernel,
+        out_shape=[
+            jax.ShapeDtypeStruct((rows, model), F32),
+            jax.ShapeDtypeStruct((rows, model), LOW),
+        ],
+        compiler_params=pltpu.CompilerParams(vmem_limit_bytes=VMEM_BYTES),
+        cost_estimate=pl.CostEstimate(
+            flops=2 * rows * model * model, bytes_accessed=rows * model * 10, transcendentals=0
+        ),
+        name="out_project",
+    )(tokens, attn, w_out, gain)
+
+
+def gate_and_slope(gate):
+    inner = 0.7978845608028654 * (gate + 0.044715 * gate * gate * gate)
+    bent = jnp.tanh(inner)
+    half = 0.5 * (1.0 + bent)
+    slope = half + 0.5 * gate * (1.0 - bent * bent) * (
+        0.7978845608028654 * (1.0 + 3.0 * 0.044715 * gate * gate)
+    )
+    return gate * half, slope
+
+
+def ffn_first_kernel(
+    nf_own_ref, nf_other_ref, dy_own_ref, dy_other_ref, gate_ref, up_ref, down_ref,
+    hidden_ref, dgate_ref, dup_ref, own_ref, other_ref,
+    nf_ref, dy_ref, total_ref,
+):
+    step = pl.program_id(0)
+    half = nf_own_ref.shape[0]
+
+    @pl.when(step == 0)
+    def _():
+        nf_ref[:half, :] = nf_own_ref[...]
+        nf_ref[half:, :] = nf_other_ref[...]
+        dy_ref[:half, :] = dy_own_ref[...]
+        dy_ref[half:, :] = dy_other_ref[...]
+        total_ref[...] = jnp.zeros_like(total_ref)
+
+    for part in range(4):
+        rows = slice(part * half // 2, (part + 1) * half // 2)
+        nf = nf_ref[rows, :]
+        gate = dot(nf, gate_ref[...])
+        up = dot(nf, up_ref[...])
+        dhidden = dot(dy_ref[rows, :], down_ref[...], NT)
+        bent, slope = gate_and_slope(gate)
+        hidden_ref[rows, :] = (bent * up).astype(LOW)
+        dgate = (dhidden * up * slope).astype(LOW)
+        dup = (dhidden * bent).astype(LOW)
+        dgate_ref[rows, :] = dgate
+        dup_ref[rows, :] = dup
+        total_ref[rows, :] += dot(dgate, gate_ref[...], NT) + dot(dup, up_ref[...], NT)
+
+    @pl.when(step == pl.num_programs(0) - 1)
+    def _():
+        own_ref[...] = total_ref[:half, :]
+        other_ref[...] = total_ref[half:, :].astype(LOW)
+
+
+def ffn_first(nf_own, nf_other, dy_own, dy_other, w_gate, w_up, w_down, tile):
+    half, model = nf_own.shape
+    units = w_down.shape[0]
+    per = model // tile
+    whole = pl.BlockSpec((half, model), lambda t: (0, 0))
+    lane_tile = pl.BlockSpec((2 * half, tile), lambda t: (0, t))
+    return pl.pallas_call(
+        ffn_first_kernel,
+        grid=(units // tile,),
+        in_specs=[
+            whole,
+            whole,
+            whole,
+            whole,
+            pl.BlockSpec((None, model, tile), lambda t: (t // per, 0, t % per)),
+            pl.BlockSpec((None, model, tile), lambda t: (t // per, 0, t % per)),
+            pl.BlockSpec((tile, model), lambda t: (t, 0)),
+        ],
+        out_specs=[lane_tile, lane_tile, lane_tile, whole, whole],
+        out_shape=[
+            jax.ShapeDtypeStruct((2 * half, units), LOW),
+            jax.ShapeDtypeStruct((2 * half, units), LOW),
+            jax.ShapeDtypeStruct((2 * half, units), LOW),
+            jax.ShapeDtypeStruct((half, model), F32),
+            jax.ShapeDtypeStruct((half, model), LOW),
+        ],
+        scratch_shapes=[
+            pltpu.VMEM((2 * half, model), LOW),
+            pltpu.VMEM((2 * half, model), LOW),
+            pltpu.VMEM((2 * half, model), F32),
+        ],
+        compiler_params=pltpu.CompilerParams(vmem_limit_bytes=VMEM_BYTES),
+        cost_estimate=pl.CostEstimate(
+            flops=2 * 5 * 2 * half * model * units,
+            bytes_accessed=6 * model * units + 12 * half * units + 20 * half * model,
+            transcendentals=2 * half * units,
+        ),
+        name="ffn_first",
+    )(nf_own, nf_other, dy_own, dy_other, w_gate, w_up, w_down)
+
+
+def out_back_kernel(
+    own_ref, recv_ref, res_ref, dy_ref, gain_ref, w_ref, dattn_ref, dres_ref, branch_ref, dgain_ref
+):
+    chips = dattn_ref.shape[0] // 2
+    width = dattn_ref.shape[3]
+    grad = own_ref[...] + recv_ref[...].astype(F32)
+    residual = res_ref[...]
+    scale = rms_rows(residual)
+    unit = residual * scale
+    dgain_ref[...] = jnp.sum(grad * unit, axis=0, keepdims=True)
+    inner = grad * gain_ref[...]
+    dres = dy_ref[...].astype(F32) + scale * (
+        inner - unit * jnp.mean(inner * unit, axis=-1, keepdims=True)
+    )
+    dres_ref[...] = dres
+    branch = dres.astype(LOW)
+    branch_ref[...] = branch
+    for chip in range(chips):
+        part = dot(branch, w_ref[chip * width : (chip + 1) * width, :], NT).astype(LOW)
+        dattn_ref[2 * chip : 2 * chip + 2] = part.reshape(2, *dattn_ref.shape[1:])
+
+
+def out_back(own, recv, residual, dy, gain, w_out, attn_shape):
+    rows, model = own.shape
+    return pl.pallas_call(
+        out_back_kernel,
+        out_shape=[
+            jax.ShapeDtypeStruct(attn_shape, LOW),
+            jax.ShapeDtypeStruct((rows, model), F32),
+            jax.ShapeDtypeStruct((rows, model), LOW),
+            jax.ShapeDtypeStruct((1, model), F32),
+        ],
+        compiler_params=pltpu.CompilerParams(vmem_limit_bytes=VMEM_BYTES),
+        cost_estimate=pl.CostEstimate(
+            flops=2 * rows * model * model, bytes_accessed=rows * model * 20, transcendentals=0
+        ),
+        name="out_back",
+    )(own, recv, residual, dy, gain, w_out)
+
+
+def ffn_second_kernel(
+    nf_own_ref, nf_other_ref, dy_own_ref, dy_other_ref, hidden_ref, dgate_ref, dup_ref, down_ref,
+    attn_ref, branch_ref,
+    own_ref, other_ref, gdown_ref, ggate_ref, gup_ref, gout_ref,
+    nft_ref, dy_ref, total_ref,
+):
+    step = pl.program_id(0)
+    half = nf_own_ref.shape[0]
+
+    @pl.when(step == 0)
+    def _():
+        nft_ref[:, :half] = jnp.transpose(nf_own_ref[...])
+        nft_ref[:, half:] = jnp.transpose(nf_other_ref[...])
+        dy_ref[:half, :] = dy_own_ref[...]
+        dy_ref[half:, :] = dy_other_ref[...]
+        total_ref[...] = jnp.zeros_like(total_ref)
+        chips, width = attn_ref.shape[0] // 2, attn_ref.shape[3]
+        for chip in range(chips):
+            part = attn_ref[2 * chip : 2 * chip + 2].reshape(half, width)
+            gout_ref[chip * width : (chip + 1) * width, :] = dot(
+                jnp.transpose(part), branch_ref[...]
+            ).astype(LOW)
+
+    hidden = hidden_ref[...]
+    ggate_ref[...] = dot(nft_ref[...], dgate_ref[...]).astype(LOW)
+    gup_ref[...] = dot(nft_ref[...], dup_ref[...]).astype(LOW)
+    gdown_ref[...] = dot(jnp.transpose(hidden), dy_ref[...]).astype(LOW)
+    total_ref[...] += dot(hidden, down_ref[...])
+
+    @pl.when(step == pl.num_programs(0) - 1)
+    def _():
+        own_ref[...] = total_ref[:half, :]
+        other_ref[...] = total_ref[half:, :].astype(LOW)
+
+
+def ffn_second(nf_own, nf_other, dy_own, dy_other, hidden, dgate, dup, w_down, attn, branch, tile):
+    half, model = nf_own.shape
+    units = hidden.shape[1]
+    whole = pl.BlockSpec((half, model), lambda t: (0, 0))
+    lane_tile = pl.BlockSpec((2 * half, tile), lambda t: (0, t))
+    row_tile = pl.BlockSpec((tile, model), lambda t: (t, 0))
+    per = model // tile
+    out_tile = pl.BlockSpec((None, model, tile), lambda t: (t // per, 0, t % per))
+    return pl.pallas_call(
+        ffn_second_kernel,
+        grid=(units // tile,),
+        in_specs=[
+            whole, whole, whole, whole, lane_tile, lane_tile, lane_tile, row_tile,
+            pl.BlockSpec(attn.shape, lambda t: (0, 0, 0, 0)),
+            whole,
+        ],
+        out_specs=[
+            whole, whole, row_tile, out_tile, out_tile,
+            pl.BlockSpec((model, model), lambda t: (0, 0)),
+        ],
+        out_shape=[
+            jax.ShapeDtypeStruct((half, model), F32),
+            jax.ShapeDtypeStruct((half, model), LOW),
+            jax.ShapeDtypeStruct((units, model), LOW),
+            jax.ShapeDtypeStruct((units // model, model, model), LOW),
+            jax.ShapeDtypeStruct((units // model, model, model), LOW),
+            jax.ShapeDtypeStruct((model, model), LOW),
+        ],
+        scratch_shapes=[
+            pltpu.VMEM((model, 2 * half), LOW),
+            pltpu.VMEM((2 * half, model), LOW),
+            pltpu.VMEM((2 * half, model), F32),
+        ],
+        compiler_params=pltpu.CompilerParams(vmem_limit_bytes=VMEM_BYTES),
+        cost_estimate=pl.CostEstimate(
+            flops=2 * 4 * 2 * half * model * units,
+            bytes_accessed=8 * model * units + 12 * half * units + 20 * half * model,
+            transcendentals=0,
+        ),
+        name="ffn_second",
+    )(nf_own, nf_other, dy_own, dy_other, hidden, dgate, dup, w_down, attn, branch)
+
+
+CORE, X, Y = 1, 2, 4
+
+
+def swap(values, bit):
+    count = lax.axis_size("ctx")
+    return lax.ppermute(values, "ctx", [(i, i ^ bit) for i in range(count)])
+
+
+def ring_step(values):
+    count = lax.axis_size("fsdp")
+    return lax.ppermute(values, "fsdp", [(i, (i + 1) % count) for i in range(count)])
+
+
+def bit_of(bit):
+    return (lax.axis_index("ctx") // bit) % 2
+
+
+def pick(values, index, axis):
+    return lax.dynamic_index_in_dim(values, index, axis, keepdims=False)
+
+
+def put_in_order(mine, other, bit, axis=0):
+    first = bit_of(bit) == 0
+    return jnp.stack([jnp.where(first, mine, other), jnp.where(first, other, mine)], axis)
+
+
+def halve_sum(values, bit, axis):
+    side = bit_of(bit)
+    kept = pick(values, side, axis)
+    came = swap(pick(values, 1 - side, axis), bit)
+    return (kept.astype(F32) + came.astype(F32)).astype(LOW)
+
+
+def ring_sum(values, axis):
+    count = lax.axis_size("fsdp")
+    me = lax.axis_index("fsdp")
+    running = pick(values, (me + count - 1) % count, axis)
+    for step in range(count - 1):
+        came = ring_step(running)
+        mine = pick(values, (me + 2 * count - 2 - step) % count, axis)
+        running = (came.astype(F32) + mine.astype(F32)).astype(LOW)
+    return running
+
+
+def ring_pieces(piece):
+    count = lax.axis_size("fsdp")
+    me = lax.axis_index("fsdp")
+    found = []
+    for step in range(count - 1):
+        piece = ring_step(piece)
+        found.append(((me + 2 * count - 1 - step) % count, piece))
+    return found
+
+
+def place(whole, piece, owner):
+    return lax.dynamic_update_slice_in_dim(whole, piece[None], owner, 0)
+
+
+def per_device_plane(
+    tokens, cotangent, lengths, bucket_table, gain_attn, w_query, w_key, w_value, w_out,
+    bias_table, gain_ffn, w_gate, w_up, w_ffn_out,
+):
+    batch, rows, model = tokens.shape
+    planes = lax.axis_size("fsdp")
+    chips = lax.axis_size("ctx") // 2
+    seq = rows * chips * 2
+    me = lax.axis_index("ctx")
+    plane = lax.axis_index("fsdp")
+    core, chip = me % 2, me // 2
+    depth = model // planes
+    units = w_gate.shape[1]
+    chip_heads = HEADS // chips
+    width = chip_heads * HEAD_DIM
+    half_rows = batch * rows
+
+    order = jnp.argsort(-lengths)
+    order = jnp.stack([order[0], order[3], order[1], order[2]])
+    lens = lengths[order]
+    local = jnp.concatenate([pick(tokens, order[i], 0)[None] for i in range(batch)])
+    grads_in = jnp.concatenate([pick(cotangent, order[i], 0)[None] for i in range(batch)])
+    positions = me * rows + jnp.arange(rows, dtype=jnp.int32)
+    valid = positions[None, :] < lens[:, None]
+    dy = jnp.where(valid[..., None], grads_in, jnp.zeros_like(grads_in)).reshape(half_rows, model)
+    flat = local.reshape(half_rows, model)
+    lens_mine = lax.dynamic_slice_in_dim(lens, 2 * core, 2)
+
+    by_core = local.reshape(2, 2, rows, model)
+    came = swap(pick(by_core, 1 - core, 0), CORE)
+    block = put_in_order(pick(by_core, core, 0), came, CORE, 1).reshape(2, 2 * rows, model)
+    from_x = swap(block, X)
+    from_y = swap(block, Y)
+    from_xy = jnp.stack([swap(from_x[0], Y), swap(from_y[1], X)])
+    by_distance = jnp.stack([block, from_x, from_y, from_xy])
+    gathered = jnp.concatenate(
+        [pick(by_distance, chip ^ i, 0) for i in range(chips)], axis=1
+    )
+
+    small = jnp.concatenate([gain_attn, gain_ffn, bias_table.reshape(-1)])[None]
+    all_small = jnp.zeros((planes, 1, small.shape[1]), LOW)
+    all_small = place(all_small, small, plane)
+    for owner, piece in ring_pieces(small):
+        all_small = place(all_small, piece, owner)
+    all_small = all_small[:, 0]
+    full_gain_attn = all_small[:, :depth].reshape(1, model).astype(F32)
+    full_gain_ffn = all_small[:, depth : 2 * depth].reshape(1, model).astype(F32)
+    full_table = all_small[:, 2 * depth :].reshape(BUCKETS, HEADS)
+
+    qkv_piece = jnp.stack(
+        [
+            lax.dynamic_slice_in_dim(w, chip * width, width, 1)
+            for w in (w_query, w_key, w_value)
+        ]
+    )
+    w_qkv = jnp.zeros((planes, 3, depth, width), LOW)
+    w_qkv = place(w_qkv, qkv_piece, plane)
+    for owner, piece in ring_pieces(qkv_piece):
+        w_qkv = place(w_qkv, piece, owner)
+    w_qkv = jnp.transpose(w_qkv, (1, 0, 2, 3)).reshape(3, model, width)
+
+    out_halves = w_out.reshape(2, depth // 2, model)
+    half_out = jnp.zeros((planes, depth // 2, model), LOW)
+    mine = pick(out_halves, core, 0)
+    half_out = place(half_out, mine, plane)
+    for owner, piece in ring_pieces(mine):
+        half_out = place(half_out, piece, owner)
+    full_out = put_in_order(half_out, swap(half_out, CORE), CORE, 1).reshape(model, model)
+
+    part = units // planes // 2
+    wide = units // 2 // model
+
+    def my_columns(w):
+        mine = pick(w.reshape(depth, planes, 2, part), core, 2).reshape(depth, wide, model)
+        return jnp.transpose(mine, (1, 0, 2))
+
+    gate_mine, up_mine = my_columns(w_gate), my_columns(w_up)
+    down_mine = pick(w_ffn_out.reshape(2, part, model), core, 0)
+    down_two = down_mine.reshape(2, part // 2, model)
+    slab = depth // 2
+    x_piece = jnp.concatenate(
+        [
+            pick(gate_mine.reshape(wide, 2, slab, model), bit_of(X), 1).reshape(-1, model),
+            pick(down_two[0].reshape(2, part // 4, model), bit_of(X), 0),
+        ]
+    )
+    y_piece = jnp.concatenate(
+        [
+            pick(up_mine.reshape(wide, 2, slab, model), bit_of(Y), 1).reshape(-1, model),
+            pick(down_two[1].reshape(2, part // 4, model), bit_of(Y), 0),
+        ]
+    )
+    full_gate = place(jnp.zeros((planes, wide, depth, model), LOW), gate_mine, plane)
+    full_up = place(jnp.zeros((planes, wide, depth, model), LOW), up_mine, plane)
+    full_down = place(jnp.zeros((planes, 2, part // 2, model), LOW), down_two, plane)
+    x_found, y_found = ring_pieces(x_piece), ring_pieces(y_piece)
+    for (owner, from_ring), (_, from_ring_y) in zip(x_found, y_found):
+        both_x = put_in_order(from_ring, swap(from_ring, X), X)
+        both_y = put_in_order(from_ring_y, swap(from_ring_y, Y), Y)
+        cut = wide * slab
+
+        def columns(both):
+            return jnp.transpose(both[:, :cut].reshape(2, wide, slab, model), (1, 0, 2, 3)).reshape(
+                wide, depth, model
+            )
+
+        full_gate = place(full_gate, columns(both_x), owner)
+        full_up = place(full_up, columns(both_y), owner)
+        full_down = place(
+            full_down,
+            jnp.stack(
+                [
+                    both_x[:, cut:].reshape(part // 2, model),
+                    both_y[:, cut:].reshape(part // 2, model),
+                ]
+            ),
+            owner,
+        )
+    full_gate = jnp.transpose(full_gate, (1, 0, 2, 3)).reshape(wide, model, model)
+    full_up = jnp.transpose(full_up, (1, 0, 2, 3)).reshape(wide, model, model)
+    full_down = full_down.reshape(units // 2, model)
+
+    hot = (bucket_table[:, None] == jnp.arange(BUCKETS, dtype=jnp.int32)[None, :])
+    hot = jnp.concatenate([hot, jnp.zeros((1, BUCKETS), bool)])
+    my_table = lax.dynamic_slice_in_dim(full_table, chip * chip_heads, chip_heads, 1)
+    offsets = jnp.einsum("tb,bh->ht", hot.astype(LOW), my_table, preferred_element_type=F32)
+
+    attn_out, attn_full, lse, query, key, value = attn_forward(
+        lens_mine, gathered, full_gain_attn, w_qkv, offsets, 2 * chips
+    )
+    attn = lax.all_to_all(attn_out, "ctx", 0, 0)
+    residual, nf_own = out_project(flat, attn, full_out, full_gain_ffn)
+    dy_other = swap(dy, CORE)
+    nf_other = swap(nf_own, CORE)
+    hidden, dgate, dup, dnf_own, dnf_send = ffn_first(
+        nf_own, nf_other, dy, dy_other, full_gate, full_up, full_down, TILE
+    )
+    dattn, dres, branch, dgain_ffn = out_back(
+        dnf_own, swap(dnf_send, CORE), residual, dy, full_gain_ffn, full_out, attn.shape
+    )
+    dattn_all = lax.all_to_all(dattn, "ctx", 0, 0)
+    out_own, out_send, gdown, ggate, gup, gout = ffn_second(
+        nf_own, nf_other, dy, dy_other, hidden, dgate, dup, full_down, attn, branch, TILE
+    )
+    out_rows = residual + out_own + swap(out_send, CORE).astype(F32)
+    out_rows = jnp.where(valid[..., None], out_rows.reshape(batch, rows, model), 0.0).astype(LOW)
+
+    quarter = depth // 4
+    g_sum = ring_sum(ggate.reshape(wide, planes, depth, model), 1)
+    g_sum = halve_sum(g_sum.reshape(wide, 2, 2, quarter, model), X, 1)
+    g_sum = halve_sum(g_sum, Y, 1)
+    u_sum = halve_sum(gup.reshape(wide, planes, 2, 2, quarter, model), X, 2)
+    u_sum = ring_sum(halve_sum(u_sum, Y, 2), 1)
+    f_sum = halve_sum(gdown.reshape(planes, 2, 2, part // 4, model), Y, 1)
+    f_sum = ring_sum(halve_sum(f_sum, X, 1), 0)
+    o_sum = halve_sum(gout.reshape(planes, 2, 2, 2, depth // 8, model), CORE, 1)
+    o_sum = ring_sum(halve_sum(halve_sum(o_sum, X, 1), Y, 1), 0)
+
+    dn_all, dw_qkv, dgain_attn, doffsets = attn_backward(
+        lens_mine, gathered, full_gain_attn, w_qkv, offsets,
+        query, key, value, attn_full, lse, dattn_all,
+    )
+
+    dn = dn_all.reshape(2, 2, 2, 2 * rows, model)
+    dn_x = halve_sum(halve_sum(dn[:, :, 0], X, 1), Y, 0)
+    dn_y = halve_sum(halve_sum(dn[:, :, 1], Y, 0), X, 0)
+    dn = jnp.stack([dn_x, dn_y]).reshape(2, 2, rows, model)
+    dn_came = swap(pick(dn, 1 - core, 1), CORE)
+    dn_rows = put_in_order(pick(dn, core, 1), dn_came, CORE).reshape(half_rows, model)
+    dn_rows = dn_rows.astype(F32)
+    rows_f = flat.astype(F32)
+    scale = rms_rows(rows_f)
+    unit = rows_f * scale
+    inner = dn_rows * full_gain_attn
+    dtok = dres + scale * (inner - unit * jnp.mean(inner * unit, axis=-1, keepdims=True))
+    dtok = dtok.reshape(batch, rows, model)
+
+    dw = jnp.transpose(dw_qkv.astype(LOW)).reshape(planes, 2, depth // 2, 3 * width)
+    dw = ring_sum(halve_sum(dw, CORE, 1), 0)
+    dw = put_in_order(dw, swap(dw, X), X)
+    dw = put_in_order(dw, swap(dw, Y), Y)
+    dw = put_in_order(dw, swap(dw, CORE), CORE).reshape(2, chips, depth // 2, 3, width)
+    dw = jnp.transpose(dw, (3, 0, 2, 1, 4)).reshape(3, depth, model).astype(F32)
+
+    pack_x = jnp.concatenate([g_sum.reshape(-1, model), u_sum[0].reshape(-1, model)])
+    pack_y = jnp.concatenate(
+        [u_sum[1:].reshape(-1, model), f_sum.reshape(-1, model), o_sum.reshape(-1, model)]
+    )
+    pack_x = put_in_order(pack_x, swap(pack_x, X), X)
+    pack_x = put_in_order(pack_x, swap(pack_x, Y), Y)
+    pack_y = put_in_order(pack_y, swap(pack_y, Y), Y)
+    pack_y = put_in_order(pack_y, swap(pack_y, X), X, 1)
+    pack = jnp.concatenate([pack_x, pack_y], axis=2)
+    gate_rows = wide * quarter
+    down_at = 2 * gate_rows
+    out_at = down_at + part // 4
+    pack = put_in_order(pack, swap(pack, CORE), CORE)
+
+    def columns_of(gathered_rows):
+        cut = gathered_rows.reshape(2, 2, 2, wide, quarter, planes // wide, part)
+        cut = jnp.transpose(cut, (2, 1, 4, 3, 5, 0, 6))
+        return cut.reshape(depth, units).astype(F32)
+
+    grad_gate = columns_of(pack[:, :, :, :gate_rows])
+    grad_up = columns_of(pack[:, :, :, gate_rows:down_at])
+    grad_down = jnp.transpose(pack[:, :, :, down_at:out_at], (0, 1, 2, 3, 4))
+    grad_down = grad_down.reshape(units // planes, model).astype(F32)
+    grad_out = jnp.transpose(pack[:, :, :, out_at:], (0, 2, 1, 3, 4))
+    grad_out = grad_out.reshape(depth, model).astype(F32)
+
+    mine_buckets = jnp.einsum(
+        "ht,tb->bh", doffsets, hot.astype(F32), precision=lax.Precision.HIGHEST
+    )
+    buckets = lax.dynamic_update_slice_in_dim(
+        jnp.zeros((BUCKETS, HEADS), F32), mine_buckets, chip * chip_heads, 1
+    )
+    sums = jnp.concatenate([dgain_attn[0], dgain_ffn[0], buckets.reshape(-1)])
+    sums = lax.psum(sums, ("ctx", "fsdp"))
+    grad_gain_attn = lax.dynamic_slice_in_dim(sums, plane * depth, depth)
+    grad_gain_ffn = lax.dynamic_slice_in_dim(sums, model + plane * depth, depth)
+    grad_buckets = lax.dynamic_slice_in_dim(
+        sums[2 * model :].reshape(BUCKETS, HEADS), plane * (BUCKETS // planes), BUCKETS // planes
+    )
+
+    back = jnp.argsort(order)
+    out_rows = jnp.concatenate([pick(out_rows, back[i], 0)[None] for i in range(batch)])
+    dtok = jnp.concatenate([pick(dtok, back[i], 0)[None] for i in range(batch)])
+    return (
+        out_rows, dtok, grad_gain_attn, dw[0], dw[1], dw[2], grad_out, grad_buckets,
+        grad_gain_ffn, grad_gate, grad_up, grad_down,
+    )
 
 
 def gelu_tanh(values):
@@ -95,7 +957,7 @@
     return lax.fori_loop(0, block_count, advance, carried)
 
 
-def per_device(
+def per_device_general(
     tokens,
     cotangent,
     lengths,
@@ -448,8 +1310,9 @@
         P("fsdp", None),
         P("fsdp", None),
     )
+    plane = mesh.shape["ctx"] == 8 and mesh.shape["fsdp"] == 4
     return jax.shard_map(
-        per_device,
+        per_device_plane if plane else per_device_general,
         mesh=mesh,
         in_specs=placed,
         out_specs=(

time: 1660 us -> 566 us (0.34)
  the two profiles are of different devices: /device:TPU:9 before, /device:TPU:0 now
where the time goes in v1:
time: 566 us; the launch traced here: 555 us
  waiting for transfers between devices  179 us (32%)
  local copies, waits for them, and re-layouts  113 us (20%)
  Pallas kernels  92.7 us (16%)
  starting transfers between devices  58.2 us (10%)
  other arithmetic  54.4 us (10%)
  blocking collectives  39.2 us (7%)
  between operations  17.9 us (3%)
    ppermute x30, waiting for transfers between devices, ring_step(): lax.ppermute(values, 'fsdp', [(i, (i + 1) % count) for i in range(count)])  92.1 us
    ppermute x39, waiting for transfers between devices, swap(): return lax.ppermute(values, 'ctx', [(i, i ^ bit) for i in range(count)])  57.9 us
    psum x1, blocking collectives, per_device_plane(): sums = lax.psum(sums, ('ctx', 'fsdp'))  39.2 us
    ppermute x39, starting transfers between devices, swap(): return lax.ppermute(values, 'ctx', [(i, i ^ bit) for i in range(count)])  37.7 us
    pallas_call x1, Pallas kernels, attn_backward(): pl.pallas_call(attn_backward_kernel, grid=(slots,), in_specs=[pl.BlockSpe...  24.6 us
    pallas_call x1, Pallas kernels, ffn_first(): pl.pallas_call(ffn_first_kernel, grid=(units // tile,), in_specs=[whole,...  22.7 us
    all_to_all x1, waiting for transfers between devices, per_device_plane(): dattn_all = lax.all_to_all(dattn, 'ctx', 0, 0)  22.5 us
    convert_element_type x6, local copies, waits for them, and re-layouts, columns_of(): return cut.reshape(depth, units).astype(F32)  20.7 us
  transfers between devices with their start and end apart: 71, of which 33 were waited for; matrix products, arithmetic and copies ran while one was open for 21% of the time, Pallas kernels for 8%

profile of v1, /device:TPU:0, one launch (start us, length us, event | category | flops | bytes accessed | tf_op | source)
XLA Modules:
  0.0 555.5 jit_solution(1884102389139797415)
XLA Ops:
  0.7 3.4 reshape.538
  4.1 3.3 reshape.547
  7.4 8.1 %dynamic-slice_reduce_fusion = (bf16[192,4,384]{2,1,0:T(4,128)(2,1)}, bf16[192,4,384]{2,1,0:T(4,128)(2,1)S(1)}) fusion(bf16[192,4,2,384]{3,2,1,0:T(2,128)(2,1)S(1)} %reshape.547, s32[]{:T(128)S(6)} %select_n.605, bf16[192,4,2,384]{3,2,1,0:T(2,128)(2,1)S(1)} %reshape.538), kind=kLoop, calls=%fused_computation.49 | loop fusion | bytes 2359300 | tf_op jit(solution)/shard_map/jit(dynamic_index_in_dim)/dynamic_slice | solution.py:605
  18.8 3.2 collective-permute-start.23
  54.2 3.9 collective-permute-done.6
  58.9 4.6 collective-permute-done.7
  67.7 6.5 %collective-permute-done.8 = bf16[3,192,192]{2,1,0:T(8,128)(2,1)} collective-permute-done((bf16[3,192,192]{2,1,0:T(8,128)(2,1)}, bf16[3,192,192]{2,1,0:T(8,128)(2,1)}, u32[]{:S(2)}, u32[]{:S(2)}) %collective-permute-start.8) | collective-permute-done | bytes 221216 | tf_op jit(solution)/shard_map/ppermute | solution.py:597
  80.7 2.7 collective-permute-done.9
  87.7 6.5 %collective-permute-done.10 = bf16[3,192,192]{2,1,0:T(8,128)(2,1)S(1)} collective-permute-done((bf16[3,192,192]{2,1,0:T(8,128)(2,1)S(1)}, bf16[3,192,192]{2,1,0:T(8,128)(2,1)S(1)}, u32[]{:S(2)}, u32[]{:S(2)}) %collective-permute-start.10) | collective-permute-done | bytes 221216 | tf_op jit(solution)/shard_map/ppermute | solution.py:597
  96.4 11.0 %collective-permute-done.24 = bf16[288,768]{1,0:T(8,128)(2,1)S(1)} collective-permute-done((bf16[288,768]{1,0:T(8,128)(2,1)}, bf16[288,768]{1,0:T(8,128)(2,1)S(1)}, u32[]{:S(2)}, u32[]{:S(2)}) %collective-permute-start.24) | collective-permute-done | bytes 442400 | tf_op jit(solution)/shard_map/ppermute | solution.py:592
  111.7 8.8 %collective-permute-done.19 = bf16[288,768]{1,0:T(8,128)(2,1)} collective-permute-done((bf16[288,768]{1,0:T(8,128)(2,1)}, bf16[288,768]{1,0:T(8,128)(2,1)}, u32[]{:S(2)}, u32[]{:S(2)}) %collective-permute-start.19) | collective-permute-done | bytes 442400 | tf_op jit(solution)/shard_map/ppermute | solution.py:597
  127.2 8.4 %collective-permute-done.26 = bf16[288,768]{1,0:T(8,128)(2,1)S(1)} collective-permute-done((bf16[288,768]{1,0:T(8,128)(2,1)S(1)}, bf16[288,768]{1,0:T(8,128)(2,1)S(1)}, u32[]{:S(2)}, u32[]{:S(2)}) %collective-permute-start.26) | collective-permute-done | bytes 442400 | tf_op jit(solution)/shard_map/ppermute | solution.py:592
  139.8 7.3 %collective-permute-done.27 = bf16[288,768]{1,0:T(8,128)(2,1)} collective-permute-done((bf16[288,768]{1,0:T(8,128)(2,1)S(1)}, bf16[288,768]{1,0:T(8,128)(2,1)}, u32[]{:S(2)}, u32[]{:S(2)}) %collective-permute-start.27) | collective-permute-done | bytes 442400 | tf_op jit(solution)/shard_map/ppermute | solution.py:597
  152.8 17.5 %attn_forward.1 = (bf16[8,2,128,192]{3,2,1,0:T(8,128)(2,1)}, f32[2,1024,192]{2,1,0:T(8,128)}, f32[2,3,1024,128]{3,2,1,0:T(8,128)}, bf16[2,1024,192]{2,1,0:T(8,12...) custom-call(s32[2]{0:T(128)} %dynamic_slice.295.lens_ref, ...), custom_call_target="tpu_custom_call" | custom-call | flops 8254390272 | bytes 9437184 | tf_op jit(solution)/shard_map/attn_forward/pallas_call | solution.py:150
  170.3 2.2 copy.155
  172.5 4.4 all-to-all-start
  183.7 6.2 %all-to-all-done = bf16[8,2,128,192]{2,3,1,0:T(8,128)(2,1)} async-done(((bf16[8,2,128,192]{2,3,1,0:T(8,128)(2,1)}), bf16[8,2,128,192]{2,3,1,0:T(8,128)(2,1)}, u32[]{:S(2)}, u32[]{:S(2)}) %all-to-all-start) | async-done | bytes 786464 | tf_op jit(solution)/shard_map/all_to_all | solution.py:775
  189.9 2.2 copy.157.attn_ref
  192.2 4.3 out_project.1
  200.2 3.2 copy.164
  205.3 22.7 %ffn_first.1 = (bf16[1024,1536]{1,0:T(8,128)(2,1)}, bf16[1024,1536]{1,0:T(8,128)(2,1)}, bf16[1024,1536]{1,0:T(8,128)(2,1)}, f32[512,768]{1,0:T(8,128)}, bf16[512,768]{1,0:T(8,128)(2,1)}) custom-call(bf16[512,768]{1,0:T(8,128)(2,1)} %get-tuple-element.44.nf_own_ref, bf16[512,768]{1,0:T(8,128)(2,1)} %copy-done.39, ...), custom_call_target="tpu_custom_call" | custom-call | flops 12079595520 | bytes 24379392 | tf_op jit(solution)/shard_map/ffn_first/pallas_call | solution.py:434
  228.2 2.4 collective-permute-done.29.recv_ref
  231.5 5.5 out_back.1
  237.0 18.0 %ffn_second.1 = (f32[512,768]{1,0:T(8,128)}, bf16[512,768]{1,0:T(8,128)(2,1)}, bf16[1536,768]{1,0:T(8,128)(2,1)}, bf16[2,768,768]{2,1,0:T(8,128)(2,1)}, bf16[2,7...) custom-call(bf16[512,768]{1,0:T(8,128)(2,1)} %get-tuple-element.44.nf_own_ref, bf16[512,768]{1,0:T(8,128)(2,1)} %copy-done.39, ...), custom_call_target="tpu_custom_call" | custom-call | flops 9663676416 | bytes 26738688 | tf_op jit(solution)/shard_map/ffn_second/pallas_call | solution.py:552
  271.2 2.4 copy.173
  273.6 3.8 all-to-all-start.1
  280.6 2.2 fusion.16
  286.8 22.5 %all-to-all-done.1 = bf16[8,2,128,192]{2,3,1,0:T(8,128)(2,1)S(1)} async-done(((bf16[8,2,128,192]{2,3,1,0:T(8,128)(2,1)}), bf16[8,2,128,192]{2,3,1,0:T(8,128)(2,1)S(1)}, u32[]{:S(2)}, u32[]{:S(2)}) %all-to-all-start.1) | async-done | bytes 786464 | tf_op jit(solution)/shard_map/all_to_all | solution.py:785
  310.6 24.6 %attn_backward.1 = (bf16[4,2,256,768]{3,2,1,0:T(8,128)(2,1)}, f32[576,768]{1,0:T(8,128)}, f32[1,768]{1,0:T(1,128)}, f32[3,2048]{1,0:T(4,128)}) custom-call(s32[2]{0:T(128)} %dynamic_slice.295.lens_ref, bf16[2,1024,768]{2,1,0:T(8,128)(2,1)} %pad_maximum_fusion.1.tok_ref, f32[1,768]{1,0:T(1,128)} %reshape.569.gain_ref, bf16[3,768,192]{2,1,0:T(8,128)(2,1)} %bitcast.476, ...), custom_call_target="tpu_custom_call" | custom-call | flops 19730006016 | bytes 15728640 | tf_op jit(solution)/shard_map/attn_backward/pallas_call | solution.py:307
  337.7 39.2 %psum.7 = f32[1920]{0:T(1024)S(1)} all-reduce(f32[1920]{0:T(1024)S(1)} %pad_maximum_fusion.24), channel_id=1, replica_groups=mesh['ctx'=8,'fsdp'=4] {'ctx','fsdp'}, use_global_device_ids=true, to_apply=%region_4.5 | all-reduce | flops 1920 | bytes 15360 | tf_op jit(solution)/shard_map/psum | solution.py:862
  384.4 2.4 collective-permute-start.62
  387.0 2.9 collective-permute-done.62
  390.0 2.2 collective-permute-start.63
  392.2 3.5 collective-permute-done.63
  397.5 4.1 collective-permute-done.64
  401.6 2.1 collective-permute-start.33
  404.0 5.9 %collective-permute-done.65 = bf16[24,768]{1,0:T(8,128)(2,1)S(1)} collective-permute-done((bf16[24,768]{1,0:T(8,128)(2,1)S(1)}, bf16[24,768]{1,0:T(8,128)(2,1)S(1)}, u32[]{:S(2)}, u32[]{:S(2)}) %collective-permute-start.65) | collective-permute-done | bytes 36896 | tf_op jit(solution)/shard_map/ppermute | solution.py:597
  413.8 4.9 collective-permute-done.37
  421.7 6.3 %collective-permute-done.38 = bf16[96,576]{1,0:T(8,128)(2,1)S(1)} collective-permute-done((bf16[96,576]{1,0:T(8,128)(2,1)S(1)}, bf16[96,576]{1,0:T(8,128)(2,1)S(1)}, u32[]{:S(2)}, u32[]{:S(2)}) %collective-permute-start.38) | collective-permute-done | bytes 110624 | tf_op jit(solution)/shard_map/ppermute | solution.py:597
  428.1 6.6 %collective-permute-done.39 = bf16[96,576]{1,0:T(8,128)(2,1)S(1)} collective-permute-done((bf16[96,576]{1,0:T(8,128)(2,1)S(1)}, bf16[96,576]{1,0:T(8,128)(2,1)S(1)}, u32[]{:S(2)}, u32[]{:S(2)}) %collective-permute-start.39) | collective-permute-done | bytes 110624 | tf_op jit(solution)/shard_map/ppermute | solution.py:597
  438.8 13.2 %collective-permute-done.40 = bf16[96,576]{1,0:T(8,128)(2,1)S(1)} collective-permute-done((bf16[96,576]{1,0:T(8,128)(2,1)S(1)}, bf16[96,576]{1,0:T(8,128)(2,1)S(1)}, u32[]{:S(2)}, u32[]{:S(2)}) %collective-permute-start.40) | collective-permute-done | bytes 110624 | tf_op jit(solution)/shard_map/ppermute | solution.py:592
  456.1 6.3 %collective-permute-done.41 = bf16[2,96,576]{2,1,0:T(8,128)(2,1)S(1)} collective-permute-done((bf16[2,96,576]{2,1,0:T(8,128)(2,1)S(1)}, bf16[2,96,576]{2,1,0:T(8,128)(2,1)S(1)}, u32[]{:S(2)}, u32[]{:S(2)}) %collective-permute-start.41) | collective-permute-done | bytes 221216 | tf_op jit(solution)/shard_map/ppermute | solution.py:592
  464.3 5.4 collective-permute-done.57
  470.5 2.4 collective-permute-done.51
  473.0 3.8 collective-permute-done.58
  476.9 4.5 collective-permute-done.52
  484.4 3.1 collective-permute-done.53
  488.9 4.0 collective-permute-done.66
  497.3 2.1 collective-permute-done.54
  500.5 2.8 collective-permute-done.67
  507.9 2.3 copy.179
  510.3 2.4 squeeze.241
  512.7 2.3 copy.180
  515.0 2.4 squeeze.242
  517.5 2.3 copy.181
  519.8 2.4 squeeze.243
  526.7 2.2 select_bitcast_fusion.1
  528.9 3.2 fusion.10
  532.9 2.9 reshape.607
  535.8 3.2 copy.204
  539.0 4.1 reshape.604
  543.2 2.9 reshape.608
  546.1 3.2 copy.203
  549.3 4.3 reshape.605
  (397 shorter events, 147.4 us)
Async XLA Ops:
  18.8 66.9 %collective-permute-start.23 = (bf16[288,768]{1,0:T(8,128)(2,1)}, bf16[288,768]{1,0:T(8,128)(2,1)}, u32[]{:S(2)}, u32[]{:S(2)}) collective-permute-start(bf16[288,768]{1,0:T(8,128)(2,1)} %pad_maximum_fusion.12), channel_id=1, source_target_pairs={{0,1},{1,2},{2,3},{3,0},{4,5},{5,6},{6,7},{7,4},{8,9},{9,10},{10,1... | collective-permute-start | bytes 1327112 | tf_op jit(solution)/shard_map/ppermute | solution.py:597
  23.5 64.0 %collective-permute-start.17 = (bf16[288,768]{1,0:T(8,128)(2,1)}, bf16[288,768]{1,0:T(8,128)(2,1)}, u32[]{:S(2)}, u32[]{:S(2)}) collective-permute-start(bf16[288,768]{1,0:T(8,128)(2,1)} %pad_maximum_fusion.11), channel_id=1, source_target_pairs={{0,1},{1,2},{2,3},{3,0},{4,5},{5,6},{6,7},{7,4},{8,9},{9,10},{10,1... | collective-permute-start | bytes 1327112 | tf_op jit(solution)/shard_map/ppermute | solution.py:597
  26.8 39.3 %collective-permute-start.11 = (bf16[96,768]{1,0:T(8,128)(2,1)}, bf16[96,768]{1,0:T(8,128)(2,1)}, u32[]{:S(2)}, u32[]{:S(2)}) collective-permute-start(bf16[96,768]{1,0:T(8,128)(2,1)} %get-tuple-element.134), channel_id=1, source_target_pairs={{0,1},{1,2},{2,3},{3,0},{4,5},{5,6},{6,7},{7,4},{8,9},{9,10},{10,1... | collective-permute-start | bytes 442376 | tf_op jit(solution)/shard_map/ppermute | solution.py:597
  39.5 38.4 %collective-permute-start = (bf16[2,128,768]{2,1,0:T(8,128)(2,1)}, bf16[2,128,768]{2,1,0:T(8,128)(2,1)}, u32[]{:S(2)}, u32[]{:S(2)}) collective-permute-start(bf16[2,128,768]{2,1,0:T(8,128)(2,1)} %dynamic-slice_bitcast_fusion.15), channel_id=1, source_target_pairs={{0,4},{4,0},{8,12},{12,8},{16,20},{20,16},{24,28},{28,24},{1,5},{5... | collective-permute-start | bytes 1179656 | tf_op jit(solution)/shard_map/ppermute | solution.py:592
  39.7 13.1 %collective-permute-start.5 = (bf16[1,480]{1,0:T(2,128)(2,1)S(1)}, bf16[1,480]{1,0:T(2,128)(2,1)S(1)}, u32[]{:S(2)}, u32[]{:S(2)}) collective-permute-start(bf16[1,480]{1,0:T(2,128)(2,1)S(1)} %squeeze.223), channel_id=1, source_target_pairs={{0,1},{1,2},{2,3},{3,0},{4,5},{5,6},{6,7},{7,4},{8,9},{9,10},{10,1... | collective-permute-start | bytes 2888 | tf_op jit(solution)/shard_map/ppermute | solution.py:597
  63.5 10.6 %collective-permute-start.8 = (bf16[3,192,192]{2,1,0:T(8,128)(2,1)}, bf16[3,192,192]{2,1,0:T(8,128)(2,1)}, u32[]{:S(2)}, u32[]{:S(2)}) collective-permute-start(bf16[3,192,192]{2,1,0:T(8,128)(2,1)} %pad_maximum_fusion.20), channel_id=1, source_target_pairs={{0,1},{1,2},{2,3},{3,0},{4,5},{5,6},{6,7},{7,4},{8,9},{9,10},{10,1... | collective-permute-start | bytes 663560 | tf_op jit(solution)/shard_map/ppermute | solution.py:597
  66.0 11.2 %collective-permute-start.12 = (bf16[96,768]{1,0:T(8,128)(2,1)}, bf16[96,768]{1,0:T(8,128)(2,1)S(1)}, u32[]{:S(2)}, u32[]{:S(2)}) collective-permute-start(bf16[96,768]{1,0:T(8,128)(2,1)} %collective-permute-done.11), channel_id=1, source_target_pairs={{0,1},{1,2},{2,3},{3,0},{4,5},{5,6},{6,7},{7,4},{8,9},{9,10},{10,1... | collective-permute-start | bytes 442376 | tf_op jit(solution)/shard_map/ppermute | solution.py:597
  74.2 9.2 %collective-permute-start.9 = (bf16[3,192,192]{2,1,0:T(8,128)(2,1)}, bf16[3,192,192]{2,1,0:T(8,128)(2,1)S(1)}, u32[]{:S(2)}, u32[]{:S(2)}) collective-permute-start(bf16[3,192,192]{2,1,0:T(8,128)(2,1)} %collective-permute-done.8), channel_id=1, source_target_pairs={{0,1},{1,2},{2,3},{3,0},{4,5},{5,6},{6,7},{7,4},{8,9},{9,10},{10,1... | collective-permute-start | bytes 663560 | tf_op jit(solution)/shard_map/ppermute | solution.py:597
  77.2 8.5 %collective-permute-start.13 = (bf16[96,768]{1,0:T(8,128)(2,1)S(1)}, bf16[96,768]{1,0:T(8,128)(2,1)S(1)}, u32[]{:S(2)}, u32[]{:S(2)}) collective-permute-start(bf16[96,768]{1,0:T(8,128)(2,1)S(1)} %collective-permute-done.12), channel_id=1, source_target_pairs={{0,1},{1,2},{2,3},{3,0},{4,5},{5,6},{6,7},{7,4},{8,9},{9,10},{10,1... | collective-permute-start | bytes 442376 | tf_op jit(solution)/shard_map/ppermute | solution.py:597
  79.1 46.0 %collective-permute-start.1 = (bf16[2,256,768]{2,1,0:T(8,128)(2,1)S(1)}, bf16[2,256,768]{2,1,0:T(8,128)(2,1)S(1)}, u32[]{:S(2)}, u32[]{:S(2)}) collective-permute-start(bf16[2,256,768]{2,1,0:T(8,128)(2,1)S(1)} %bitcast.436), channel_id=1, source_target_pairs={{0,8},{4,12},{8,0},{12,4},{16,24},{20,28},{24,16},{28,20},{1,9},{5... | collective-permute-start | bytes 2359304 | tf_op jit(solution)/shard_map/ppermute | solution.py:592
  83.4 43.3 %collective-permute-start.2 = (bf16[2,256,768]{2,1,0:T(8,128)(2,1)S(1)}, bf16[2,256,768]{2,1,0:T(8,128)(2,1)S(1)}, u32[]{:S(2)}, u32[]{:S(2)}) collective-permute-start(bf16[2,256,768]{2,1,0:T(8,128)(2,1)S(1)} %bitcast.437), channel_id=1, source_target_pairs={{0,16},{4,20},{8,24},{12,28},{16,0},{20,4},{24,8},{28,12},{1,17},{... | collective-permute-start | bytes 2359304 | tf_op jit(solution)/shard_map/ppermute | solution.py:592
  85.7 8.5 %collective-permute-start.10 = (bf16[3,192,192]{2,1,0:T(8,128)(2,1)S(1)}, bf16[3,192,192]{2,1,0:T(8,128)(2,1)S(1)}, u32[]{:S(2)}, u32[]{:S(2)}) collective-permute-start(bf16[3,192,192]{2,1,0:T(8,128)(2,1)S(1)} %collective-permute-done.9), channel_id=1, source_target_pairs={{0,1},{1,2},{2,3},{3,0},{4,5},{5,6},{6,7},{7,4},{8,9},{9,10},{10,1... | collective-permute-start | bytes 663560 | tf_op jit(solution)/shard_map/ppermute | solution.py:597
  85.7 21.7 %collective-permute-start.24 = (bf16[288,768]{1,0:T(8,128)(2,1)}, bf16[288,768]{1,0:T(8,128)(2,1)S(1)}, u32[]{:S(2)}, u32[]{:S(2)}) collective-permute-start(bf16[288,768]{1,0:T(8,128)(2,1)} %collective-permute-done.23), channel_id=1, source_target_pairs={{0,16},{4,20},{8,24},{12,28},{16,0},{20,4},{24,8},{28,12},{1,17},{... | collective-permute-start | bytes 1327112 | tf_op jit(solution)/shard_map/ppermute | solution.py:592
  87.6 32.9 %collective-permute-start.14 = (bf16[4,96,768]{2,1,0:T(8,128)(2,1)S(1)}, bf16[4,96,768]{2,1,0:T(8,128)(2,1)S(1)}, u32[]{:S(2)}, u32[]{:S(2)}) collective-permute-start(bf16[4,96,768]{2,1,0:T(8,128)(2,1)S(1)} %bitcast_dynamic-update-slice_fusion.4), channel_id=1, source_target_pairs={{0,4},{4,0},{8,12},{12,8},{16,20},{20,16},{24,28},{28,24},{1,5},{5... | collective-permute-start | bytes 1769480 | tf_op jit(solution)/shard_map/ppermute | solution.py:592
  94.2 14.4 %collective-permute-start.18 = (bf16[288,768]{1,0:T(8,128)(2,1)}, bf16[288,768]{1,0:T(8,128)(2,1)S(1)}, u32[]{:S(2)}, u32[]{:S(2)}) collective-permute-start(bf16[288,768]{1,0:T(8,128)(2,1)} %collective-permute-done.17), channel_id=1, source_target_pairs={{0,8},{4,12},{8,0},{12,4},{16,24},{20,28},{24,16},{28,20},{1,9},{5... | collective-permute-start | bytes 1327112 | tf_op jit(solution)/shard_map/ppermute | solution.py:592
  107.4 13.1 %collective-permute-start.19 = (bf16[288,768]{1,0:T(8,128)(2,1)}, bf16[288,768]{1,0:T(8,128)(2,1)}, u32[]{:S(2)}, u32[]{:S(2)}) collective-permute-start(bf16[288,768]{1,0:T(8,128)(2,1)} %collective-permute-done.17), channel_id=1, source_target_pairs={{0,1},{1,2},{2,3},{3,0},{4,5},{5,6},{6,7},{7,4},{8,9},{9,10},{10,1... | collective-permute-start | bytes 1327112 | tf_op jit(solution)/shard_map/ppermute | solution.py:597
  108.6 16.5 %collective-permute-start.25 = (bf16[288,768]{1,0:T(8,128)(2,1)}, bf16[288,768]{1,0:T(8,128)(2,1)S(1)}, u32[]{:S(2)}, u32[]{:S(2)}) collective-permute-start(bf16[288,768]{1,0:T(8,128)(2,1)} %collective-permute-done.23), channel_id=1, source_target_pairs={{0,1},{1,2},{2,3},{3,0},{4,5},{5,6},{6,7},{7,4},{8,9},{9,10},{10,1... | collective-permute-start | bytes 1327112 | tf_op jit(solution)/shard_map/ppermute | solution.py:597
  120.5 83.9 %collective-permute-start.16 = (bf16[512,768]{1,0:T(8,128)(2,1)}, bf16[512,768]{1,0:T(8,128)(2,1)}, u32[]{:S(2)}, u32[]{:S(2)}) collective-permute-start(bf16[512,768]{1,0:T(8,128)(2,1)} %bitcast_select_fusion.dy_own_ref.dy_ref), channel_id=1, source_target_pairs={{0,4},{4,0},{8,12},{12,8},{16,20},{20,16},{24,28},{28,24},{1,5},{5... | collective-permute-start | bytes 2359304 | tf_op jit(solution)/shard_map/ppermute | solution.py:592
  120.5 16.7 %collective-permute-start.20 = (bf16[288,768]{1,0:T(8,128)(2,1)}, bf16[288,768]{1,0:T(8,128)(2,1)S(1)}, u32[]{:S(2)}, u32[]{:S(2)}) collective-permute-start(bf16[288,768]{1,0:T(8,128)(2,1)} %collective-permute-done.19), channel_id=1, source_target_pairs={{0,8},{4,12},{8,0},{12,4},{16,24},{20,28},{24,16},{28,20},{1,9},{5... | collective-permute-start | bytes 1327112 | tf_op jit(solution)/shard_map/ppermute | solution.py:592
  125.1 51.8 %collective-permute-start.21 = (bf16[288,768]{1,0:T(8,128)(2,1)}, bf16[288,768]{1,0:T(8,128)(2,1)}, u32[]{:S(2)}, u32[]{:S(2)}) collective-permute-start(bf16[288,768]{1,0:T(8,128)(2,1)} %collective-permute-done.19), channel_id=1, source_target_pairs={{0,1},{1,2},{2,3},{3,0},{4,5},{5,6},{6,7},{7,4},{8,9},{9,10},{10,1... | collective-permute-start | bytes 1327112 | tf_op jit(solution)/shard_map/ppermute | solution.py:597
  125.1 10.5 %collective-permute-start.26 = (bf16[288,768]{1,0:T(8,128)(2,1)S(1)}, bf16[288,768]{1,0:T(8,128)(2,1)S(1)}, u32[]{:S(2)}, u32[]{:S(2)}) collective-permute-start(bf16[288,768]{1,0:T(8,128)(2,1)S(1)} %collective-permute-done.25), channel_id=1, source_target_pairs={{0,16},{4,20},{8,24},{12,28},{16,0},{20,4},{24,8},{28,12},{1,17},{... | collective-permute-start | bytes 1327112 | tf_op jit(solution)/shard_map/ppermute | solution.py:592
  126.7 20.4 %collective-permute-start.27 = (bf16[288,768]{1,0:T(8,128)(2,1)S(1)}, bf16[288,768]{1,0:T(8,128)(2,1)}, u32[]{:S(2)}, u32[]{:S(2)}) collective-permute-start(bf16[288,768]{1,0:T(8,128)(2,1)S(1)} %collective-permute-done.25), channel_id=1, source_target_pairs={{0,1},{1,2},{2,3},{3,0},{4,5},{5,6},{6,7},{7,4},{8,9},{9,10},{10,1... | collective-permute-start | bytes 1327112 | tf_op jit(solution)/shard_map/ppermute | solution.py:597
  135.6 14.6 %collective-permute-start.3 = (bf16[256,768]{1,0:T(8,128)(2,1)S(1)}, bf16[256,768]{1,0:T(8,128)(2,1)S(1)}, u32[]{:S(2)}, u32[]{:S(2)}) collective-permute-start(bf16[256,768]{1,0:T(8,128)(2,1)S(1)} %slice_bitcast_fusion.1), channel_id=1, source_target_pairs={{0,16},{4,20},{8,24},{12,28},{16,0},{20,4},{24,8},{28,12},{1,17},{... | collective-permute-start | bytes 1179656 | tf_op jit(solution)/shard_map/ppermute | solution.py:592
  137.2 13.0 %collective-permute-start.4 = (bf16[256,768]{1,0:T(8,128)(2,1)S(1)}, bf16[256,768]{1,0:T(8,128)(2,1)S(1)}, u32[]{:S(2)}, u32[]{:S(2)}) collective-permute-start(bf16[256,768]{1,0:T(8,128)(2,1)S(1)} %slice_bitcast_fusion), channel_id=1, source_target_pairs={{0,8},{4,12},{8,0},{12,4},{16,24},{20,28},{24,16},{28,20},{1,9},{5... | collective-permute-start | bytes 1179656 | tf_op jit(solution)/shard_map/ppermute | solution.py:592
  147.1 33.6 %collective-permute-start.28 = (bf16[288,768]{1,0:T(8,128)(2,1)}, bf16[288,768]{1,0:T(8,128)(2,1)}, u32[]{:S(2)}, u32[]{:S(2)}) collective-permute-start(bf16[288,768]{1,0:T(8,128)(2,1)} %collective-permute-done.27), channel_id=1, source_target_pairs={{0,16},{4,20},{8,24},{12,28},{16,0},{20,4},{24,8},{28,12},{1,17},{... | collective-permute-start | bytes 1327112 | tf_op jit(solution)/shard_map/ppermute | solution.py:592
  172.5 17.5 %all-to-all-start = ((bf16[8,2,128,192]{2,3,1,0:T(8,128)(2,1)}), bf16[8,2,128,192]{2,3,1,0:T(8,128)(2,1)}, u32[]{:S(2)}, u32[]{:S(2)}) async-start(bf16[8,2,128,192]{2,3,1,0:T(8,128)(2,1)} %copy.155), calls=%async_computation | async-start | bytes 1572864 | tf_op jit(solution)/shard_map/all_to_all | solution.py:775
  176.9 21.1 %collective-permute-start.22 = (bf16[288,768]{1,0:T(8,128)(2,1)}, bf16[288,768]{1,0:T(8,128)(2,1)}, u32[]{:S(2)}, u32[]{:S(2)}) collective-permute-start(bf16[288,768]{1,0:T(8,128)(2,1)} %collective-permute-done.21), channel_id=1, source_target_pairs={{0,8},{4,12},{8,0},{12,4},{16,24},{20,28},{24,16},{28,20},{1,9},{5... | collective-permute-start | bytes 1327112 | tf_op jit(solution)/shard_map/ppermute | solution.py:592
  196.5 7.9 %collective-permute-start.15 = (bf16[512,768]{1,0:T(8,128)(2,1)}, bf16[512,768]{1,0:T(8,128)(2,1)S(1)}, u32[]{:S(2)}, u32[]{:S(2)}) collective-permute-start(bf16[512,768]{1,0:T(8,128)(2,1)} %get-tuple-element.44.nf_own_ref), channel_id=1, source_target_pairs={{0,4},{4,0},{8,12},{12,8},{16,20},{20,16},{24,28},{28,24},{1,5},{5... | collective-permute-start | bytes 2359304 | tf_op jit(solution)/shard_map/ppermute | solution.py:592
  257.1 23.4 %collective-permute-start.43 = (bf16[2,192,768]{2,1,0:T(8,128)(2,1)}, bf16[2,192,768]{2,1,0:T(8,128)(2,1)}, u32[]{:S(2)}, u32[]{:S(2)}) collective-permute-start(bf16[2,192,768]{2,1,0:T(8,128)(2,1)} %dynamic-slice_bitcast_fusion.11), channel_id=1, source_target_pairs={{0,1},{1,2},{2,3},{3,0},{4,5},{5,6},{6,7},{7,4},{8,9},{9,10},{10,1... | collective-permute-start | bytes 1769480 | tf_op jit(solution)/shard_map/ppermute | solution.py:597
  261.2 22.0 %collective-permute-start.60 = (bf16[4,2,2,24,768]{4,3,2,1,0:T(8,128)(2,1)}, bf16[4,2,2,24,768]{4,3,2,1,0:T(8,128)(2,1)}, u32[]{:S(2)}, u32[]{:S(2)}) collective-permute-start(bf16[4,2,2,24,768]{4,3,2,1,0:T(8,128)(2,1)} %dynamic-slice_bitcast_fusion.8), channel_id=1, source_target_pairs={{0,4},{4,0},{8,12},{12,8},{16,20},{20,16},{24,28},{28,24},{1,5},{5... | collective-permute-start | bytes 1769480 | tf_op jit(solution)/shard_map/ppermute | solution.py:592
  270.8 141.1 %collective-permute-start.48 = (bf16[2,4,2,48,768]{4,3,2,1,0:T(8,128)(2,1)}, bf16[2,4,2,48,768]{4,3,2,1,0:T(8,128)(2,1)}, u32[]{:S(2)}, u32[]{:S(2)}) collective-permute-start(bf16[2,4,2,48,768]{4,3,2,1,0:T(8,128)(2,1)} %dynamic-slice_bitcast_fusion.1), channel_id=1, source_target_pairs={{0,8},{4,12},{8,0},{12,4},{16,24},{20,28},{24,16},{28,20},{1,9},{5... | collective-permute-start | bytes 3538952 | tf_op jit(solution)/shard_map/ppermute | solution.py:592
  273.6 35.7 %all-to-all-start.1 = ((bf16[8,2,128,192]{2,3,1,0:T(8,128)(2,1)}), bf16[8,2,128,192]{2,3,1,0:T(8,128)(2,1)S(1)}, u32[]{:S(2)}, u32[]{:S(2)}) async-start(bf16[8,2,128,192]{2,3,1,0:T(8,128)(2,1)} %copy.173), calls=%async_computation.1 | async-start | bytes 1572864 | tf_op jit(solution)/shard_map/all_to_all | solution.py:785
  278.5 141.5 %collective-permute-start.55 = (bf16[4,2,96,768]{3,2,1,0:T(8,128)(2,1)}, bf16[4,2,96,768]{3,2,1,0:T(8,128)(2,1)}, u32[]{:S(2)}, u32[]{:S(2)}) collective-permute-start(bf16[4,2,96,768]{3,2,1,0:T(8,128)(2,1)} %dynamic-slice_bitcast_fusion), channel_id=1, source_target_pairs={{0,16},{4,20},{8,24},{12,28},{16,0},{20,4},{24,8},{28,12},{1,17},{... | collective-permute-start | bytes 3538952 | tf_op jit(solution)/shard_map/ppermute | solution.py:592
  280.5 100.8 %collective-permute-start.30 = (bf16[512,768]{1,0:T(8,128)(2,1)}, bf16[512,768]{1,0:T(8,128)(2,1)S(1)}, u32[]{:S(2)}, u32[]{:S(2)}) collective-permute-start(bf16[512,768]{1,0:T(8,128)(2,1)} %get-tuple-element.52), channel_id=1, source_target_pairs={{0,4},{4,0},{8,12},{12,8},{16,20},{20,16},{24,28},{28,24},{1,5},{5... | collective-permute-start | bytes 2359304 | tf_op jit(solution)/shard_map/ppermute | solution.py:592
  282.8 127.8 %collective-permute-start.44 = (bf16[2,192,768]{2,1,0:T(8,128)(2,1)}, bf16[2,192,768]{2,1,0:T(8,128)(2,1)}, u32[]{:S(2)}, u32[]{:S(2)}) collective-permute-start(bf16[2,192,768]{2,1,0:T(8,128)(2,1)} %fusion.16), channel_id=1, source_target_pairs={{0,1},{1,2},{2,3},{3,0},{4,5},{5,6},{6,7},{7,4},{8,9},{9,10},{10,1... | collective-permute-start | bytes 1769480 | tf_op jit(solution)/shard_map/ppermute | solution.py:597
  285.3 98.1 %collective-permute-start.61 = (bf16[4,2,24,768]{3,2,1,0:T(8,128)(2,1)}, bf16[4,2,24,768]{3,2,1,0:T(8,128)(2,1)}, u32[]{:S(2)}, u32[]{:S(2)}) collective-permute-start(bf16[4,2,24,768]{3,2,1,0:T(8,128)(2,1)} %dynamic-slice_bitcast_fusion.16), channel_id=1, source_target_pairs={{0,8},{4,12},{8,0},{12,4},{16,24},{20,28},{24,16},{28,20},{1,9},{5... | collective-permute-start | bytes 884744 | tf_op jit(solution)/shard_map/ppermute | solution.py:592
  381.3 22.4 %collective-permute-start.36 = (bf16[4,96,576]{2,1,0:T(8,128)(2,1)S(1)}, bf16[4,96,576]{2,1,0:T(8,128)(2,1)S(1)}, u32[]{:S(2)}, u32[]{:S(2)}) collective-permute-start(bf16[4,96,576]{2,1,0:T(8,128)(2,1)S(1)} %dynamic-slice_bitcast_fusion.12), channel_id=1, source_target_pairs={{0,4},{4,0},{8,12},{12,8},{16,20},{20,16},{24,28},{28,24},{1,5},{5... | collective-permute-start | bytes 1327112 | tf_op jit(solution)/shard_map/ppermute | solution.py:592
  401.6 34.5 %collective-permute-start.33 = (bf16[2,256,768]{2,1,0:T(8,128)(2,1)S(1)}, bf16[2,256,768]{2,1,0:T(8,128)(2,1)S(1)}, u32[]{:S(2)}, u32[]{:S(2)}) collective-permute-start(bf16[2,256,768]{2,1,0:T(8,128)(2,1)S(1)} %dynamic-slice_bitcast_fusion.2), channel_id=1, source_target_pairs={{0,16},{4,20},{8,24},{12,28},{16,0},{20,4},{24,8},{28,12},{1,17},{... | collective-permute-start | bytes 2359304 | tf_op jit(solution)/shard_map/ppermute | solution.py:592
  403.8 6.2 %collective-permute-start.65 = (bf16[24,768]{1,0:T(8,128)(2,1)S(1)}, bf16[24,768]{1,0:T(8,128)(2,1)S(1)}, u32[]{:S(2)}, u32[]{:S(2)}) collective-permute-start(bf16[24,768]{1,0:T(8,128)(2,1)S(1)} %fusion.52), channel_id=1, source_target_pairs={{0,1},{1,2},{2,3},{3,0},{4,5},{5,6},{6,7},{7,4},{8,9},{9,10},{10,1... | collective-permute-start | bytes 110600 | tf_op jit(solution)/shard_map/ppermute | solution.py:597
  409.9 27.2 %collective-permute-start.31 = (bf16[2,256,768]{2,1,0:T(8,128)(2,1)S(1)}, bf16[2,256,768]{2,1,0:T(8,128)(2,1)S(1)}, u32[]{:S(2)}, u32[]{:S(2)}) collective-permute-start(bf16[2,256,768]{2,1,0:T(8,128)(2,1)S(1)} %dynamic-slice_bitcast_fusion.3), channel_id=1, source_target_pairs={{0,8},{4,12},{8,0},{12,4},{16,24},{20,28},{24,16},{28,20},{1,9},{5... | collective-permute-start | bytes 2359304 | tf_op jit(solution)/shard_map/ppermute | solution.py:592
  410.5 8.1 %collective-permute-start.37 = (bf16[96,576]{1,0:T(8,128)(2,1)S(1)}, bf16[96,576]{1,0:T(8,128)(2,1)S(1)}, u32[]{:S(2)}, u32[]{:S(2)}) collective-permute-start(bf16[96,576]{1,0:T(8,128)(2,1)S(1)} %dynamic-slice_bitcast_fusion.25), channel_id=1, source_target_pairs={{0,1},{1,2},{2,3},{3,0},{4,5},{5,6},{6,7},{7,4},{8,9},{9,10},{10,1... | collective-permute-start | bytes 331784 | tf_op jit(solution)/shard_map/ppermute | solution.py:597
  411.9 40.7 %collective-permute-start.45 = (bf16[2,192,768]{2,1,0:T(8,128)(2,1)S(1)}, bf16[2,192,768]{2,1,0:T(8,128)(2,1)S(1)}, u32[]{:S(2)}, u32[]{:S(2)}) collective-permute-start(bf16[2,192,768]{2,1,0:T(8,128)(2,1)S(1)} %fusion.15), channel_id=1, source_target_pairs={{0,1},{1,2},{2,3},{3,0},{4,5},{5,6},{6,7},{7,4},{8,9},{9,10},{10,1... | collective-permute-start | bytes 1769480 | tf_op jit(solution)/shard_map/ppermute | solution.py:597
  418.7 35.7 %collective-permute-start.49 = (bf16[2,4,48,768]{3,2,1,0:T(8,128)(2,1)S(1)}, bf16[2,4,48,768]{3,2,1,0:T(8,128)(2,1)S(1)}, u32[]{:S(2)}, u32[]{:S(2)}) collective-permute-start(bf16[2,4,48,768]{3,2,1,0:T(8,128)(2,1)S(1)} %dynamic-slice_bitcast_fusion.10), channel_id=1, source_target_pairs={{0,16},{4,20},{8,24},{12,28},{16,0},{20,4},{24,8},{28,12},{1,17},{... | collective-permute-start | bytes 1769480 | tf_op jit(solution)/shard_map/ppermute | solution.py:592
  420.0 8.0 %collective-permute-start.38 = (bf16[96,576]{1,0:T(8,128)(2,1)S(1)}, bf16[96,576]{1,0:T(8,128)(2,1)S(1)}, u32[]{:S(2)}, u32[]{:S(2)}) collective-permute-start(bf16[96,576]{1,0:T(8,128)(2,1)S(1)} %fusion.50), channel_id=1, source_target_pairs={{0,1},{1,2},{2,3},{3,0},{4,5},{5,6},{6,7},{7,4},{8,9},{9,10},{10,1... | collective-permute-start | bytes 331784 | tf_op jit(solution)/shard_map/ppermute | solution.py:597
  428.0 6.7 %collective-permute-start.39 = (bf16[96,576]{1,0:T(8,128)(2,1)S(1)}, bf16[96,576]{1,0:T(8,128)(2,1)S(1)}, u32[]{:S(2)}, u32[]{:S(2)}) collective-permute-start(bf16[96,576]{1,0:T(8,128)(2,1)S(1)} %fusion.49), channel_id=1, source_target_pairs={{0,1},{1,2},{2,3},{3,0},{4,5},{5,6},{6,7},{7,4},{8,9},{9,10},{10,1... | collective-permute-start | bytes 331784 | tf_op jit(solution)/shard_map/ppermute | solution.py:597
  434.7 21.1 %collective-permute-start.56 = (bf16[4,96,768]{2,1,0:T(8,128)(2,1)S(1)}, bf16[4,96,768]{2,1,0:T(8,128)(2,1)S(1)}, u32[]{:S(2)}, u32[]{:S(2)}) collective-permute-start(bf16[4,96,768]{2,1,0:T(8,128)(2,1)S(1)} %dynamic-slice_bitcast_fusion.9), channel_id=1, source_target_pairs={{0,8},{4,12},{8,0},{12,4},{16,24},{20,28},{24,16},{28,20},{1,9},{5... | collective-permute-start | bytes 1769480 | tf_op jit(solution)/shard_map/ppermute | solution.py:592
  436.1 15.9 %collective-permute-start.40 = (bf16[96,576]{1,0:T(8,128)(2,1)S(1)}, bf16[96,576]{1,0:T(8,128)(2,1)S(1)}, u32[]{:S(2)}, u32[]{:S(2)}) collective-permute-start(bf16[96,576]{1,0:T(8,128)(2,1)S(1)} %fusion.48), channel_id=1, source_target_pairs={{0,8},{4,12},{8,0},{12,4},{16,24},{20,28},{24,16},{28,20},{1,9},{5... | collective-permute-start | bytes 331784 | tf_op jit(solution)/shard_map/ppermute | solution.py:592
  437.1 25.4 %collective-permute-start.34 = (bf16[256,768]{1,0:T(8,128)(2,1)S(1)}, bf16[256,768]{1,0:T(8,128)(2,1)S(1)}, u32[]{:S(2)}, u32[]{:S(2)}) collective-permute-start(bf16[256,768]{1,0:T(8,128)(2,1)S(1)} %dynamic-slice_bitcast_fusion.13), channel_id=1, source_target_pairs={{0,8},{4,12},{8,0},{12,4},{16,24},{20,28},{24,16},{28,20},{1,9},{5... | collective-permute-start | bytes 1179656 | tf_op jit(solution)/shard_map/ppermute | solution.py:592
  452.0 10.8 %collective-permute-start.32 = (bf16[256,768]{1,0:T(8,128)(2,1)S(1)}, bf16[256,768]{1,0:T(8,128)(2,1)S(1)}, u32[]{:S(2)}, u32[]{:S(2)}) collective-permute-start(bf16[256,768]{1,0:T(8,128)(2,1)S(1)} %dynamic-slice_bitcast_fusion.14), channel_id=1, source_target_pairs={{0,16},{4,20},{8,24},{12,28},{16,0},{20,4},{24,8},{28,12},{1,17},{... | collective-permute-start | bytes 1179656 | tf_op jit(solution)/shard_map/ppermute | solution.py:592
  452.6 9.8 %collective-permute-start.41 = (bf16[2,96,576]{2,1,0:T(8,128)(2,1)S(1)}, bf16[2,96,576]{2,1,0:T(8,128)(2,1)S(1)}, u32[]{:S(2)}, u32[]{:S(2)}) collective-permute-start(bf16[2,96,576]{2,1,0:T(8,128)(2,1)S(1)} %pad_maximum_fusion.22), channel_id=1, source_target_pairs={{0,16},{4,20},{8,24},{12,28},{16,0},{20,4},{24,8},{28,12},{1,17},{... | collective-permute-start | bytes 663560 | tf_op jit(solution)/shard_map/ppermute | solution.py:592
  454.4 15.4 %collective-permute-start.46 = (bf16[2,2,48,768]{3,2,1,0:T(8,128)(2,1)S(1)}, bf16[2,2,48,768]{3,2,1,0:T(8,128)(2,1)S(1)}, u32[]{:S(2)}, u32[]{:S(2)}) collective-permute-start(bf16[2,2,48,768]{3,2,1,0:T(8,128)(2,1)S(1)} %dynamic-slice_bitcast_fusion.17), channel_id=1, source_target_pairs={{0,8},{4,12},{8,0},{12,4},{16,24},{20,28},{24,16},{28,20},{1,9},{5... | collective-permute-start | bytes 884744 | tf_op jit(solution)/shard_map/ppermute | solution.py:592
  455.9 8.3 %collective-permute-start.50 = (bf16[2,48,768]{2,1,0:T(8,128)(2,1)S(1)}, bf16[2,48,768]{2,1,0:T(8,128)(2,1)S(1)}, u32[]{:S(2)}, u32[]{:S(2)}) collective-permute-start(bf16[2,48,768]{2,1,0:T(8,128)(2,1)S(1)} %dynamic-slice_bitcast_fusion.20), channel_id=1, source_target_pairs={{0,1},{1,2},{2,3},{3,0},{4,5},{5,6},{6,7},{7,4},{8,9},{9,10},{10,1... | collective-permute-start | bytes 442376 | tf_op jit(solution)/shard_map/ppermute | solution.py:597
  462.4 7.3 %collective-permute-start.57 = (bf16[96,768]{1,0:T(8,128)(2,1)S(1)}, bf16[96,768]{1,0:T(8,128)(2,1)S(1)}, u32[]{:S(2)}, u32[]{:S(2)}) collective-permute-start(bf16[96,768]{1,0:T(8,128)(2,1)S(1)} %dynamic-slice_bitcast_fusion.19), channel_id=1, source_target_pairs={{0,1},{1,2},{2,3},{3,0},{4,5},{5,6},{6,7},{7,4},{8,9},{9,10},{10,1... | collective-permute-start | bytes 442376 | tf_op jit(solution)/shard_map/ppermute | solution.py:597
  462.6 32.5 %collective-permute-start.42 = (bf16[2,2,96,576]{3,2,1,0:T(8,128)(2,1)S(1)}, bf16[2,2,96,576]{3,2,1,0:T(8,128)(2,1)S(1)}, u32[]{:S(2)}, u32[]{:S(2)}) collective-permute-start(bf16[2,2,96,576]{3,2,1,0:T(8,128)(2,1)S(1)} %pad_maximum_fusion.10), channel_id=1, source_target_pairs={{0,4},{4,0},{8,12},{12,8},{16,20},{20,16},{24,28},{28,24},{1,5},{5... | collective-permute-start | bytes 1327112 | tf_op jit(solution)/shard_map/ppermute | solution.py:592
  463.7 58.5 %collective-permute-start.35 = (bf16[2,128,768]{2,1,0:T(8,128)(2,1)}, bf16[2,128,768]{2,1,0:T(8,128)(2,1)}, u32[]{:S(2)}, u32[]{:S(2)}) collective-permute-start(bf16[2,128,768]{2,1,0:T(8,128)(2,1)} %fusion.35), channel_id=1, source_target_pairs={{0,4},{4,0},{8,12},{12,8},{16,20},{20,16},{24,28},{28,24},{1,5},{5... | collective-permute-start | bytes 1179656 | tf_op jit(solution)/shard_map/ppermute | solution.py:592
  464.2 8.6 %collective-permute-start.51 = (bf16[2,48,768]{2,1,0:T(8,128)(2,1)S(1)}, bf16[2,48,768]{2,1,0:T(8,128)(2,1)S(1)}, u32[]{:S(2)}, u32[]{:S(2)}) collective-permute-start(bf16[2,48,768]{2,1,0:T(8,128)(2,1)S(1)} %fusion.46), channel_id=1, source_target_pairs={{0,1},{1,2},{2,3},{3,0},{4,5},{5,6},{6,7},{7,4},{8,9},{9,10},{10,1... | collective-permute-start | bytes 442376 | tf_op jit(solution)/shard_map/ppermute | solution.py:597
  469.8 7.0 %collective-permute-start.58 = (bf16[96,768]{1,0:T(8,128)(2,1)S(1)}, bf16[96,768]{1,0:T(8,128)(2,1)S(1)}, u32[]{:S(2)}, u32[]{:S(2)}) collective-permute-start(bf16[96,768]{1,0:T(8,128)(2,1)S(1)} %fusion.43), channel_id=1, source_target_pairs={{0,1},{1,2},{2,3},{3,0},{4,5},{5,6},{6,7},{7,4},{8,9},{9,10},{10,1... | collective-permute-start | bytes 442376 | tf_op jit(solution)/shard_map/ppermute | solution.py:597
  470.0 6.9 %collective-permute-start.47 = (bf16[2,48,768]{2,1,0:T(8,128)(2,1)S(1)}, bf16[2,48,768]{2,1,0:T(8,128)(2,1)S(1)}, u32[]{:S(2)}, u32[]{:S(2)}) collective-permute-start(bf16[2,48,768]{2,1,0:T(8,128)(2,1)S(1)} %dynamic-slice_bitcast_fusion.21), channel_id=1, source_target_pairs={{0,16},{4,20},{8,24},{12,28},{16,0},{20,4},{24,8},{28,12},{1,17},{... | collective-permute-start | bytes 442376 | tf_op jit(solution)/shard_map/ppermute | solution.py:592
  472.9 8.5 %collective-permute-start.52 = (bf16[2,48,768]{2,1,0:T(8,128)(2,1)S(1)}, bf16[2,48,768]{2,1,0:T(8,128)(2,1)S(1)}, u32[]{:S(2)}, u32[]{:S(2)}) collective-permute-start(bf16[2,48,768]{2,1,0:T(8,128)(2,1)S(1)} %fusion.45), channel_id=1, source_target_pairs={{0,1},{1,2},{2,3},{3,0},{4,5},{5,6},{6,7},{7,4},{8,9},{9,10},{10,1... | collective-permute-start | bytes 442376 | tf_op jit(solution)/shard_map/ppermute | solution.py:597
  476.8 7.0 %collective-permute-start.59 = (bf16[96,768]{1,0:T(8,128)(2,1)S(1)}, bf16[96,768]{1,0:T(8,128)(2,1)S(1)}, u32[]{:S(2)}, u32[]{:S(2)}) collective-permute-start(bf16[96,768]{1,0:T(8,128)(2,1)S(1)} %fusion.42), channel_id=1, source_target_pairs={{0,1},{1,2},{2,3},{3,0},{4,5},{5,6},{6,7},{7,4},{8,9},{9,10},{10,1... | collective-permute-start | bytes 442376 | tf_op jit(solution)/shard_map/ppermute | solution.py:597
  483.9 9.1 %collective-permute-start.66 = (bf16[168,768]{1,0:T(8,128)(2,1)S(1)}, bf16[168,768]{1,0:T(8,128)(2,1)S(1)}, u32[]{:S(2)}, u32[]{:S(2)}) collective-permute-start(bf16[168,768]{1,0:T(8,128)(2,1)S(1)} %pad_maximum_fusion.21), channel_id=1, source_target_pairs={{0,16},{4,20},{8,24},{12,28},{16,0},{20,4},{24,8},{28,12},{1,17},{... | collective-permute-start | bytes 774152 | tf_op jit(solution)/shard_map/ppermute | solution.py:592
  488.4 11.0 %collective-permute-start.54 = (bf16[2,144,768]{2,1,0:T(8,128)(2,1)}, bf16[2,144,768]{2,1,0:T(8,128)(2,1)}, u32[]{:S(2)}, u32[]{:S(2)}) collective-permute-start(bf16[2,144,768]{2,1,0:T(8,128)(2,1)} %pad_maximum_fusion.13), channel_id=1, source_target_pairs={{0,16},{4,20},{8,24},{12,28},{16,0},{20,4},{24,8},{28,12},{1,17},{... | collective-permute-start | bytes 1327112 | tf_op jit(solution)/shard_map/ppermute | solution.py:592
  493.9 9.4 %collective-permute-start.67 = (bf16[2,168,768]{2,1,0:T(8,128)(2,1)}, bf16[2,168,768]{2,1,0:T(8,128)(2,1)}, u32[]{:S(2)}, u32[]{:S(2)}) collective-permute-start(bf16[2,168,768]{2,1,0:T(8,128)(2,1)} %pad_maximum_fusion.9), channel_id=1, source_target_pairs={{0,8},{4,12},{8,0},{12,4},{16,24},{20,28},{24,16},{28,20},{1,9},{5... | collective-permute-start | bytes 1548296 | tf_op jit(solution)/shard_map/ppermute | solution.py:592
  505.8 20.9 %collective-permute-start.68 = (bf16[2,2,312,768]{3,2,0,1:T(8,128)(2,1)}, bf16[2,2,312,768]{3,2,0,1:T(8,128)(2,1)}, u32[]{:S(2)}, u32[]{:S(2)}) collective-permute-start(bf16[2,2,312,768]{3,2,0,1:T(8,128)(2,1)} %maximum_maximum_fusion), channel_id=1, source_target_pairs={{0,4},{4,0},{8,12},{12,8},{16,20},{20,16},{24,28},{28,24},{1,5},{5... | collective-permute-start | bytes 5750792 | tf_op jit(solution)/shard_map/ppermute | solution.py:592
  (47 other events, 331.2 us)
